TPU v7x, 128 devices: a whole 4x4x4 slice. The times are simulated.
128 devices in a mesh: ia: 4 (over z_lo, core), ja: 4 (over y), al: 8 (over x, z_hi).
Axes of the slice: x: 4, y: 4, z: 4 (z_hi: 2, z_lo: 2; z = z_hi * 2 + z_lo), core: 2. Of those that a mesh axis runs over, the one named last changes fastest.
Arguments:
- inputs: bfloat16 [1024, 6144], P(('ia', 'al'), 'ja'), may hold values from -6 to 6
- first_weight: bfloat16 [6144, 24576], P(('ja', 'ia'), 'al'), may hold values from -0.078125 to 0.078125
- second_weight: bfloat16 [24576, 6144], P(('al', 'ia'), 'ja'), may hold values from -0.0390625 to 0.0390625
- cotangent: bfloat16 [1024, 6144], P(('ia', 'al'), 'ja'), may hold values from -1.5 to 1.5
Outputs:
- output: bfloat16 [1024, 6144], P(('ia', 'al'), 'ja')
- input_grad: bfloat16 [1024, 6144], P(('ia', 'al'), 'ja')
- first_grad: bfloat16 [6144, 24576], P(('ja', 'ia'), 'al')
- second_grad: bfloat16 [24576, 6144], P(('al', 'ia'), 'ja')
All inputs are finite; a program needn't handle non-finite values.
Results may differ from a plain program's by a relative error of at most 0.025.
Values may be sent and summed in bfloat16 or wider, within the bound.
A program may use at most 128 MiB of HBM per device.

v0:
```python
import jax
import jax.numpy as jnp
from jax import lax
from jax.sharding import PartitionSpec as P


def gelu_parts(pre):
    scaled = pre * 0.7071067811865476
    cdf = 0.5 * (1.0 + lax.erf(scaled))
    value = pre * cdf
    slope = cdf + pre * jnp.exp(-0.5 * pre * pre) * 0.3989422804014327
    return (value, slope)


def combine_hidden(partial_value):
    return lax.psum_scatter(
        partial_value.astype(jnp.bfloat16), "ja", scatter_dimension=0, tiled=True
    ).astype(jnp.float32)


def hidden_full(local):
    return lax.all_gather(local, "ja", axis=0, tiled=True)


def shards(inputs, first_weight, second_weight, cotangent):
    gathered = lax.all_gather(inputs, "al", axis=0, tiled=True)
    weight_one = lax.all_gather(first_weight, "ia", axis=0, tiled=True)
    pre = combine_hidden(jnp.dot(gathered, weight_one, preferred_element_type=jnp.float32))
    value, slope = gelu_parts(pre)
    activ = value.astype(jnp.bfloat16)
    act_rows = hidden_full(activ)
    weight_two = lax.all_gather(second_weight, "ia", axis=0, tiled=True)
    rows = act_rows
    output = lax.psum_scatter(
        jnp.dot(rows, weight_two, preferred_element_type=jnp.float32).astype(jnp.bfloat16),
        "al",
        scatter_dimension=0,
        tiled=True,
    )
    cot_rows = lax.all_gather(cotangent, "al", axis=0, tiled=True)
    grad_part = lax.dot_general(
        cot_rows, weight_two, (((1,), (1,)), ((), ())), preferred_element_type=jnp.float32
    )
    cols = act_rows
    second_grad = lax.psum_scatter(
        lax.dot_general(
            cols, cot_rows, (((0,), (0,)), ((), ())), preferred_element_type=jnp.float32
        ).astype(jnp.bfloat16),
        "ia",
        scatter_dimension=0,
        tiled=True,
    )
    grad_pre = combine_hidden(grad_part)
    grad_hid = (grad_pre * slope).astype(jnp.bfloat16)
    grad_rows = hidden_full(grad_hid)
    rows = grad_rows
    input_grad = lax.psum_scatter(
        lax.dot_general(
            rows, weight_one, (((1,), (1,)), ((), ())), preferred_element_type=jnp.float32
        ).astype(jnp.bfloat16),
        "al",
        scatter_dimension=0,
        tiled=True,
    )
    cols = gathered
    first_grad = lax.psum_scatter(
        lax.dot_general(
            cols, grad_rows, (((0,), (0,)), ((), ())), preferred_element_type=jnp.float32
        ).astype(jnp.bfloat16),
        "ia",
        scatter_dimension=0,
        tiled=True,
    )
    return (output, input_grad, first_grad, second_grad)


def solution(mesh):
    in_specs = (
        P(("ia", "al"), "ja"),
        P(("ja", "ia"), "al"),
        P(("al", "ia"), "ja"),
        P(("ia", "al"), "ja"),
    )
    out_specs = (
        P(("ia", "al"), "ja"),
        P(("ia", "al"), "ja"),
        P(("ja", "ia"), "al"),
        P(("al", "ia"), "ja"),
    )
    return jax.shard_map(shards, mesh=mesh, in_specs=in_specs, out_specs=out_specs, check_vma=False)
```

profile of v0, /device:TPU:1, one launch (start us, length us, event | category | flops | bytes accessed | tf_op | source)
XLA Modules:
  0.0 671.7 jit_solution(13266762749034546378)
XLA Ops:
  7.2 0.7 all-gather.9.cloned.1.call-update
  8.0 0.7 all-gather.5.cloned.1.call-update
  8.7 32.2 %all_gather.22 = bf16[256,1536]{1,0:T(8,128)(2,1)S(1)} all-gather(bf16[32,1536]{1,0:T(8,128)(2,1)S(1)} %copy-done.2), channel_id=1, replica_groups=mesh['ia'=4,'ja'=4,'al'=8] {'al'}, dimensions={0}, use_global_device_ids=true | all-gather | bytes 884736 | tf_op jit(solution)/shard_map/all_gather | solution.py:40
  40.9 71.2 %all-gather.9.cloned.1.call-done = bf16[3072,1536]{1,0:T(8,128)(2,1)} async-done(((bf16[768,1536]{1,0:T(8,128)(2,1)}), bf16[3072,1536]{1,0:T(8,128)(2,1)}) %all-gather.9.cloned.1.call-update) | async-done | bytes 9437200 | tf_op jit(solution)/shard_map/all_gather | solution.py:32
  112.1 10.9 %convolution_convert_fusion.2 = bf16[256,3072]{1,0:T(8,128)(2,1)} fusion(bf16[256,1536]{1,0:T(8,128)(2,1)S(1)} %all_gather.22, bf16[3072,1536]{1,0:T(8,128)(2,1)} %all-gather.9.cloned.1.call-done), kind=kOutput, calls=%fused_computation.3 | convolution fusion | flops 2416705536 | bytes 11796480 | tf_op jit(solution)/shard_map/dot_general | solution.py:41
  123.0 32.2 %all_gather.18 = bf16[256,1536]{1,0:T(8,128)(2,1)S(1)} all-gather(bf16[32,1536]{1,0:T(8,128)(2,1)S(1)} %copy-done.3), channel_id=1, replica_groups=mesh['ia'=4,'ja'=4,'al'=8] {'al'}, dimensions={0}, use_global_device_ids=true | all-gather | bytes 884736 | tf_op jit(solution)/shard_map/all_gather | solution.py:26
  155.2 63.1 %all-gather.5.cloned.1.call-done = bf16[1536,3072]{1,0:T(8,128)(2,1)} async-done(((bf16[384,3072]{1,0:T(8,128)(2,1)}), bf16[1536,3072]{1,0:T(8,128)(2,1)}) %all-gather.5.cloned.1.call-update) | async-done | bytes 9437200 | tf_op jit(solution)/shard_map/all_gather | solution.py:27
  218.2 7.4 %convolution_convert_fusion.3 = bf16[256,3072]{1,0:T(8,128)(2,1)} fusion(bf16[256,1536]{1,0:T(8,128)(2,1)S(1)} %all_gather.18, bf16[1536,3072]{1,0:T(8,128)(2,1)} %all-gather.5.cloned.1.call-done), kind=kOutput, calls=%fused_computation.4 | convolution fusion | flops 2416705536 | bytes 11796480 | tf_op jit(solution)/shard_map/dot_general | solution.py:28
  225.7 19.6 %reduce-scatter.13.cloned.1.call-done = bf16[64,3072]{1,0:T(8,128)(2,1)} async-done(((bf16[256,3072]{1,0:T(8,128)(2,1)}), bf16[64,3072]{1,0:T(8,128)(2,1)}) %reduce-scatter.13.cloned.1.call-update) | async-done | bytes 393232 | tf_op jit(solution)/shard_map/reduce_scatter | solution.py:16
  245.3 28.4 %reduce-scatter.9.cloned.1.call-done = bf16[64,3072]{1,0:T(8,128)(2,1)} async-done(((bf16[256,3072]{1,0:T(8,128)(2,1)}), bf16[64,3072]{1,0:T(8,128)(2,1)}) %reduce-scatter.9.cloned.1.call-update) | async-done | bytes 393232 | tf_op jit(solution)/shard_map/reduce_scatter | solution.py:16
  273.6 2.4 fusion.9
  276.1 0.5 all-gather.7.cloned.1.call-update
  276.7 26.7 %all-gather.11.cloned.1.call-done = bf16[256,3072]{1,0:T(8,128)(2,1)} async-done(((bf16[64,3072]{1,0:T(8,128)(2,1)}), bf16[256,3072]{1,0:T(8,128)(2,1)}) %all-gather.11.cloned.1.call-update) | async-done | bytes 1572880 | tf_op jit(solution)/shard_map/all_gather | solution.py:22
  303.4 7.7 %convolution_convert_fusion.4 = bf16[256,1536]{1,0:T(8,128)(2,1)} fusion(bf16[256,3072]{1,0:T(8,128)(2,1)} %all-gather.11.cloned.1.call-done, bf16[1536,3072]{1,0:T(8,128)(2,1)} %all-gather.5.cloned.1.call-done), kind=kOutput, calls=%fused_computation.5 | convolution fusion | flops 2416312320 | bytes 11796480 | tf_op jit(solution)/shard_map/dot_general | solution.py:58
  311.1 20.9 %all-gather.7.cloned.1.call-done = bf16[256,3072]{1,0:T(8,128)(2,1)} async-done(((bf16[64,3072]{1,0:T(8,128)(2,1)}), bf16[256,3072]{1,0:T(8,128)(2,1)}) %all-gather.7.cloned.1.call-update) | async-done | bytes 1572880 | tf_op jit(solution)/shard_map/all_gather | solution.py:22
  332.1 7.8 %convolution_convert_fusion.5 = bf16[256,1536]{1,0:T(8,128)(2,1)} fusion(bf16[256,3072]{1,0:T(8,128)(2,1)} %all-gather.7.cloned.1.call-done, bf16[3072,1536]{1,0:T(8,128)(2,1)} %all-gather.9.cloned.1.call-done), kind=kOutput, calls=%fused_computation.6 | convolution fusion | flops 2416312320 | bytes 11796480 | tf_op jit(solution)/shard_map/dot_general | solution.py:35
  340.0 5.1 convolution_convert_fusion
  345.1 1.4 copy-done
  346.5 5.2 fusion
  351.7 12.7 %copy.10 = bf16[1536,3072]{1,0:T(8,128)(2,1)} copy(bf16[1536,3072]{0,1:T(8,128)(2,1)} %fusion) | data formatting | bytes 18874368
  364.4 42.1 %reduce-scatter.15.cloned.1.call-done = bf16[32,1536]{1,0:T(8,128)(2,1)} async-done(((bf16[256,1536]{1,0:T(8,128)(2,1)}), bf16[32,1536]{1,0:T(8,128)(2,1)}) %reduce-scatter.15.cloned.1.call-update) | async-done | bytes 98320 | tf_op jit(solution)/shard_map/reduce_scatter | solution.py:57
  406.5 75.2 %reduce-scatter.11.cloned.1.call-done = bf16[32,1536]{1,0:T(8,128)(2,1)} async-done(((bf16[256,1536]{1,0:T(8,128)(2,1)}), bf16[32,1536]{1,0:T(8,128)(2,1)}) %reduce-scatter.11.cloned.1.call-update) | async-done | bytes 98320 | tf_op jit(solution)/shard_map/reduce_scatter | solution.py:34
  481.6 91.8 %reduce-scatter.17.cloned.1.call-done = bf16[768,1536]{1,0:T(8,128)(2,1)} async-done(((bf16[3072,1536]{1,0:T(8,128)(2,1)}), bf16[768,1536]{1,0:T(8,128)(2,1)}) %reduce-scatter.17.cloned.1.call-update) | async-done | bytes 2359312 | tf_op jit(solution)/shard_map/reduce_scatter | solution.py:45
  573.4 91.5 %reduce-scatter.19.cloned.1.call-done = bf16[384,3072]{1,0:T(8,128)(2,1)} async-done(((bf16[1536,3072]{1,0:T(8,128)(2,1)}), bf16[384,3072]{1,0:T(8,128)(2,1)}) %reduce-scatter.19.cloned.1.call-update) | async-done | bytes 2359312
  (24 shorter events, 0.5 us)
Async XLA Ops:
  7.2 1.5 copy-start.2
  7.2 104.9 %all-gather.9.cloned.1.call-start = ((), (), s32[]{:S(2)}) async-start(), calls=%async_computation.9 | async-start | bytes 11796480 | tf_op jit(solution)/shard_map/all_gather | solution.py:32
  7.9 210.3 %all-gather.5.cloned.1.call-start = ((), (), s32[]{:S(2)}) async-start(), calls=%async_computation.6 | async-start | bytes 11796480 | tf_op jit(solution)/shard_map/all_gather | solution.py:27
  8.7 236.6 %reduce-scatter.13.cloned.1.call-start = ((), (), s32[]{:S(2)}) async-start(), calls=%async_computation.11 | async-start | bytes 1966080 | tf_op jit(solution)/shard_map/reduce_scatter | solution.py:16
  40.9 82.1 %copy-start.3 = (bf16[32,1536]{1,0:T(8,128)(2,1)S(1)}, bf16[32,1536]{1,0:T(8,128)(2,1)}, u32[]{:S(2)}) copy-start(bf16[32,1536]{1,0:T(8,128)(2,1)} %param.4) | copy-start | bytes 294916
  122.9 150.7 %reduce-scatter.9.cloned.1.call-start = ((), (), s32[]{:S(2)}) async-start(), calls=%async_computation.7 | async-start | bytes 1966080 | tf_op jit(solution)/shard_map/reduce_scatter | solution.py:16
  225.6 77.8 %all-gather.11.cloned.1.call-start = ((), (), s32[]{:S(2)}) async-start(), calls=%async_computation.12 | async-start | bytes 1966080 | tf_op jit(solution)/shard_map/all_gather | solution.py:22
  276.1 56.0 %all-gather.7.cloned.1.call-start = ((), (), s32[]{:S(2)}) async-start(), calls=%async_computation.8 | async-start | bytes 1966080 | tf_op jit(solution)/shard_map/all_gather | solution.py:22
  276.7 129.8 %reduce-scatter.15.cloned.1.call-start = ((), (), s32[]{:S(2)}) async-start(), calls=%async_computation.13 | async-start | bytes 884736 | tf_op jit(solution)/shard_map/reduce_scatter | solution.py:57
  311.1 170.5 %reduce-scatter.11.cloned.1.call-start = ((), (), s32[]{:S(2)}) async-start(), calls=%async_computation.10 | async-start | bytes 884736 | tf_op jit(solution)/shard_map/reduce_scatter | solution.py:34
  332.1 7.9 %copy-start.1 = (bf16[256,3072]{1,0:T(8,128)(2,1)S(1)}, bf16[256,3072]{1,0:T(8,128)(2,1)}, u32[]{:S(2)}) copy-start(bf16[256,3072]{1,0:T(8,128)(2,1)} %all-gather.7.cloned.1.call-done) | copy-start | bytes 4718596
  339.9 233.5 %reduce-scatter.17.cloned.1.call-start = ((), (), s32[]{:S(2)}) async-start(), calls=%async_computation.14 | async-start | bytes 11796480 | tf_op jit(solution)/shard_map/reduce_scatter | solution.py:45
  345.1 1.5 copy-start
  345.1 319.8 %reduce-scatter.19.cloned.1.call-start = ((), (), s32[]{:S(2)}) async-start(), calls=%async_computation.15 | async-start | bytes 11796480
Sparse Core Ops, SparseCore 0:
  9.7 102.3 all-gather.8
  113.7 104.4 all-gather.4
  221.2 24.0 reduce-scatter.12
  248.1 25.4 reduce-scatter.8
  276.2 27.1 all-gather.10
  305.5 26.5 all-gather.6
  336.3 70.1 reduce-scatter.14
  410.7 70.9 reduce-scatter.10
  484.7 88.6 reduce-scatter.16
  576.3 88.5 reduce-scatter.18
where the time goes:
time: 672 us
  waiting for transfers between devices  532 us (79%)
  blocking collectives  64.3 us (10%)
  matrix products  44 us (7%)
  between operations  14.2 us (2%)
  local copies, waits for them, and re-layouts  14.1 us (2%)
    unnamed x11, waiting for transfers between devices  93.5 us
    reduce_scatter x1, waiting for transfers between devices, shards(): lax.psum_scatter(lax.dot_general(cols, cot_rows, (((0,), (0,)), ((), ()))...  91.8 us
    reduce_scatter x1, waiting for transfers between devices, shards(): lax.psum_scatter(jnp.dot(rows, weight_two, preferred_element_type=jnp.flo...  75.2 us
    all_gather x1, waiting for transfers between devices, shards(): weight_two = lax.all_gather(second_weight, 'ia', axis=0, tiled=True)  71.2 us
    all_gather x1, waiting for transfers between devices, shards(): weight_one = lax.all_gather(first_weight, 'ia', axis=0, tiled=True)  63.1 us
    reduce_scatter x2, waiting for transfers between devices, combine_hidden(): lax.psum_scatter(partial_value.astype(jnp.bfloat16), 'ja', scatter_dimens...  48 us
    all_gather x2, waiting for transfers between devices, hidden_full(): return lax.all_gather(local, 'ja', axis=0, tiled=True)  47.6 us
    reduce_scatter x1, waiting for transfers between devices, shards(): lax.psum_scatter(lax.dot_general(rows, weight_one, (((1,), (1,)), ((), ()...  42.1 us
  transfers between devices with their start and end apart: 10, of which 10 were waited for; matrix products, arithmetic and copies ran while one was open for 8% of the time, Pallas kernels for 0%

commit v1 on v0

v1 whole, which is shorter than its diff:
```python
import jax
import jax.numpy as jnp
from jax import lax
from jax.sharding import PartitionSpec as P


def gelu_parts(pre):
    scaled = pre * 0.7071067811865476
    cdf = 0.5 * (1.0 + lax.erf(scaled))
    value = pre * cdf
    slope = cdf + pre * jnp.exp(-0.5 * pre * pre) * 0.3989422804014327
    return (value, slope)


def shards(inputs, first_weight, second_weight, cotangent):
    bf16, f32 = jnp.bfloat16, jnp.float32
    mine = lax.all_to_all(inputs, "ia", split_axis=1, concat_axis=0, tiled=True)
    tokens = lax.all_gather(mine, "al", axis=0, tiled=True)
    pre = jnp.dot(tokens, first_weight, preferred_element_type=f32).astype(bf16)
    pre = lax.psum_scatter(pre, "ia", scatter_dimension=1, tiled=True)
    pre = lax.psum_scatter(pre, "ja", scatter_dimension=0, tiled=True).astype(f32)
    cot = lax.all_gather(cotangent, ("al", "ia"), axis=0, tiled=True)
    grad_act = lax.dot_general(
        cot, second_weight, (((1,), (1,)), ((), ())), preferred_element_type=f32
    ).astype(bf16)
    grad_act = lax.psum_scatter(grad_act, "ja", scatter_dimension=0, tiled=True).astype(f32)
    value, slope = gelu_parts(pre)
    grad_hid = (grad_act * slope).astype(bf16)
    grad_hid = lax.all_gather(grad_hid, "ia", axis=1, tiled=True)
    grad_hid = lax.all_gather(grad_hid, "ja", axis=0, tiled=True)
    activ = lax.all_gather(value.astype(bf16), "ja", axis=0, tiled=True)
    output = jnp.dot(activ, second_weight, preferred_element_type=f32).astype(bf16)
    output = lax.psum_scatter(output, ("al", "ia"), scatter_dimension=0, tiled=True)
    second_grad = lax.dot_general(
        activ, cot, (((0,), (0,)), ((), ())), preferred_element_type=f32
    ).astype(bf16)
    input_grad = lax.dot_general(
        grad_hid, first_weight, (((1,), (1,)), ((), ())), preferred_element_type=f32
    ).astype(bf16)
    input_grad = lax.psum_scatter(input_grad, "al", scatter_dimension=0, tiled=True)
    input_grad = lax.all_to_all(input_grad, "ia", split_axis=0, concat_axis=1, tiled=True)
    first_grad = lax.dot_general(
        tokens, grad_hid, (((0,), (0,)), ((), ())), preferred_element_type=f32
    ).astype(bf16)
    return (output, input_grad, first_grad, second_grad)


def solution(mesh):
    in_specs = (
        P(("ia", "al"), "ja"),
        P(("ja", "ia"), "al"),
        P(("al", "ia"), "ja"),
        P(("ia", "al"), "ja"),
    )
    out_specs = (
        P(("ia", "al"), "ja"),
        P(("ia", "al"), "ja"),
        P(("ja", "ia"), "al"),
        P(("al", "ia"), "ja"),
    )
    return jax.shard_map(shards, mesh=mesh, in_specs=in_specs, out_specs=out_specs, check_vma=False)
```

time: 672 us -> 445 us (0.66)
  waiting for transfers between devices: 532 us -> 337 us
  blocking collectives: 64.3 us -> 38.7 us
  local copies, waits for them, and re-layouts: 14.1 us -> 5.85 us
    unnamed x11 -> x9, waiting for transfers between devices: 93.5 us -> 1.48 us
    all_gather x4, waiting for transfers between devices: 182 us -> 124 us  [the longest x1 66.7 us: shards(): grad_hid = lax.all_gather(grad_hid, 'ja', axis=0, tiled=True)]
    reduce_scatter x5, waiting for transfers between devices: 257 us -> 212 us  [the longest x1 65.5 us: shards(): lax.psum_scatter(output, ('al', 'ia'), scatter_dimension=0, tiled=True)]
    all_gather x2 -> x1, blocking collectives: 64.3 us -> 30.9 us  [shards(): tokens = lax.all_gather(mine, 'al', axis=0, tiled=True)]
    unnamed x9 -> x3, local copies, waits for them, and re-layouts: 14.1 us -> 4.3 us
    all_to_all x0 -> x1, blocking collectives: none -> 7.84 us  [shards(): mine = lax.all_to_all(inputs, 'ia', split_axis=1, concat_axis=0, tiled=True)]
  transfers between devices with their start and end apart: 10 -> 10, of which waited for: 10 -> 9; matrix products, arithmetic and copies ran while one was open for 8% -> 10% of each run, Pallas kernels for 0% -> 0%
where the time goes in v1:
time: 445 us; the launch traced here: 444 us
  waiting for transfers between devices  337 us (76%)
  matrix products  38.8 us (9%)
  blocking collectives  38.7 us (9%)
  between operations  15.3 us (3%)
  starting transfers between devices  6.19 us (1%)
  local copies, waits for them, and re-layouts  5.85 us (1%)
    all_gather x1, waiting for transfers between devices, shards(): grad_hid = lax.all_gather(grad_hid, 'ja', axis=0, tiled=True)  66.7 us
    reduce_scatter x1, waiting for transfers between devices, shards(): lax.psum_scatter(output, ('al', 'ia'), scatter_dimension=0, tiled=True)  65.5 us
    reduce_scatter x1, waiting for transfers between devices, shards(): pre = lax.psum_scatter(pre, 'ia', scatter_dimension=1, tiled=True)  54.3 us
    reduce_scatter x1, waiting for transfers between devices, shards(): lax.psum_scatter(input_grad, 'al', scatter_dimension=0, tiled=True)  35.9 us
    all_gather x1, blocking collectives, shards(): tokens = lax.all_gather(mine, 'al', axis=0, tiled=True)  30.9 us
    reduce_scatter x1, waiting for transfers between devices, shards(): lax.psum_scatter(grad_act, 'ja', scatter_dimension=0, tiled=True)  28.3 us
    reduce_scatter x1, waiting for transfers between devices, shards(): lax.psum_scatter(pre, 'ja', scatter_dimension=0, tiled=True).astype(f32)  27.6 us
    all_gather x1, waiting for transfers between devices, shards(): grad_hid = lax.all_gather(grad_hid, 'ia', axis=1, tiled=True)  25.6 us
  transfers between devices with their start and end apart: 10, of which 9 were waited for; matrix products, arithmetic and copies ran while one was open for 10% of the time, Pallas kernels for 0%

profile of v1, /device:TPU:1, one launch (start us, length us, event | category | flops | bytes accessed | tf_op | source)
XLA Modules:
  0.0 443.9 jit_solution(1790514725198462217)
XLA Ops:
  8.1 0.7 all-gather.7.cloned.1.call-update
  8.8 0.9 copy.21
  9.7 7.8 %all_to_all.38 = bf16[32,4,384]{2,0,1:T(8,128)(2,1)S(1)} all-to-all(bf16[32,4,384]{2,0,1:T(8,128)(2,1)S(1)} %bitcast.27), channel_id=1, replica_groups=mesh['ia'=4,'ja'=4,'al'=8] {'ia'}, dimensions={1} | all-to-all | bytes 196608 | tf_op jit(solution)/shard_map/all_to_all | solution.py:17
  17.5 30.9 %all_gather.15 = bf16[1024,384]{1,0:T(8,128)(2,1)S(1)} all-gather(bf16[128,384]{1,0:T(8,128)(2,1)S(1)} %bitcast.26), channel_id=1, replica_groups=mesh['ia'=4,'ja'=4,'al'=8] {'al'}, dimensions={0}, use_global_device_ids=true | all-gather | bytes 884736 | tf_op jit(solution)/shard_map/all_gather | solution.py:18
  48.4 5.4 %convolution_convert_fusion = bf16[1024,3072]{1,0:T(8,128)(2,1)} fusion(bf16[1024,384]{1,0:T(8,128)(2,1)S(1)} %all_gather.15, bf16[384,3072]{1,0:T(8,128)(2,1)S(1)} %copy-done), kind=kOutput, calls=%fused_computation | convolution fusion | flops 2419064832 | bytes 9437184 | tf_op jit(solution)/shard_map/dot_general | solution.py:19
  53.9 9.0 %all-gather.7.cloned.1.call-done = bf16[1024,1536]{1,0:T(8,128)(2,1)} async-done(((bf16[32,1536]{1,0:T(8,128)(2,1)}), bf16[1024,1536]{1,0:T(8,128)(2,1)}) %all-gather.7.cloned.1.call-update) | async-done | bytes 3145744 | tf_op jit(solution)/shard_map/all_gather | solution.py:22
  62.9 6.4 %convolution_convert_fusion.4 = bf16[1024,768]{1,0:T(8,128)(2,1)} fusion(bf16[1024,1536]{1,0:T(8,128)(2,1)} %all-gather.7.cloned.1.call-done, bf16[768,1536]{1,0:T(8,128)(2,1)} %param.6), kind=kOutput, calls=%fused_computation.5 | convolution fusion | flops 2416705536 | bytes 7077888 | tf_op jit(solution)/shard_map/dot_general | solution.py:23
  69.3 54.3 %reduce-scatter.6.cloned.1.call-done = bf16[1024,768]{1,0:T(8,128)(2,1)} async-done(((bf16[1024,3072]{1,0:T(8,128)(2,1)}), bf16[1024,768]{1,0:T(8,128)(2,1)}) %reduce-scatter.6.cloned.1.call-update) | async-done | bytes 1572880 | tf_op jit(solution)/shard_map/reduce_scatter | solution.py:20
  123.8 28.3 %reduce-scatter.12.cloned.1.call-done = bf16[256,768]{1,0:T(8,128)(2,1)} async-done(((bf16[1024,768]{1,0:T(8,128)(2,1)}), bf16[256,768]{1,0:T(8,128)(2,1)}) %reduce-scatter.12.cloned.1.call-update) | async-done | bytes 393232 | tf_op jit(solution)/shard_map/reduce_scatter | solution.py:26
  152.1 27.6 %reduce-scatter.8.cloned.1.call-done = bf16[256,768]{1,0:T(8,128)(2,1)} async-done(((bf16[1024,768]{1,0:T(8,128)(2,1)}), bf16[256,768]{1,0:T(8,128)(2,1)}) %reduce-scatter.8.cloned.1.call-update) | async-done | bytes 393232 | tf_op jit(solution)/shard_map/reduce_scatter | solution.py:21
  179.6 2.4 fusion.9
  182.1 25.6 %all-gather.9.cloned.1.call-done = bf16[256,3072]{1,0:T(8,128)(2,1)} async-done(((bf16[256,768]{1,0:T(8,128)(2,1)}), bf16[256,3072]{1,0:T(8,128)(2,1)}) %all-gather.9.cloned.1.call-update) | async-done | bytes 1572880 | tf_op jit(solution)/shard_map/all_gather | solution.py:29
  207.8 0.7 all-gather.5.cloned.1.call-update
  208.5 66.7 %all-gather.11.cloned.1.call-done = bf16[1024,3072]{1,0:T(8,128)(2,1)} async-done(((bf16[256,3072]{1,0:T(8,128)(2,1)}), bf16[1024,3072]{1,0:T(8,128)(2,1)}) %all-gather.11.cloned.1.call-update) | async-done | bytes 6291472 | tf_op jit(solution)/shard_map/all_gather | solution.py:30
  275.3 6.5 %convolution_convert_fusion.5 = bf16[1024,384]{1,0:T(8,128)(2,1)} fusion(bf16[1024,3072]{1,0:T(8,128)(2,1)} %all-gather.11.cloned.1.call-done, bf16[384,3072]{1,0:T(8,128)(2,1)S(1)} %copy-done), kind=kOutput, calls=%fused_computation.11 | convolution fusion | flops 2416312320 | bytes 9437184 | tf_op jit(solution)/shard_map/dot_general | solution.py:37
  281.8 22.2 %all-gather.5.cloned.1.call-done = bf16[1024,768]{1,0:T(8,128)(2,1)} async-done(((bf16[256,768]{1,0:T(8,128)(2,1)}), bf16[1024,768]{1,0:T(8,128)(2,1)}) %all-gather.5.cloned.1.call-update) | async-done | bytes 1572880 | tf_op jit(solution)/shard_map/all_gather | solution.py:31
  304.0 6.4 %convolution_convert_fusion.2 = bf16[1024,1536]{1,0:T(8,128)(2,1)} fusion(bf16[1024,768]{1,0:T(8,128)(2,1)} %all-gather.5.cloned.1.call-done, bf16[768,1536]{1,0:T(8,128)(2,1)} %param.6), kind=kOutput, calls=%fused_computation.3 | convolution fusion | flops 2417491968 | bytes 7077888 | tf_op jit(solution)/shard_map/dot_general | solution.py:32
  310.5 6.4 %convolution_convert_fusion.3 = bf16[768,1536]{1,0:T(8,128)(2,1)} fusion(bf16[1024,768]{1,0:T(8,128)(2,1)} %all-gather.5.cloned.1.call-done, bf16[1024,1536]{1,0:T(8,128)(2,1)} %all-gather.7.cloned.1.call-done), kind=kOutput, calls=%fused_computation.4 | convolution fusion | flops 2417098752 | bytes 7077888 | tf_op jit(solution)/shard_map/dot_general | solution.py:34
  316.9 35.9 %reduce-scatter.14.cloned.1.call-done = bf16[128,384]{1,0:T(8,128)(2,1)} async-done(((bf16[1024,384]{1,0:T(8,128)(2,1)}), bf16[128,384]{1,0:T(8,128)(2,1)}) %reduce-scatter.14.cloned.1.call-update) | async-done | bytes 98320 | tf_op jit(solution)/shard_map/reduce_scatter | solution.py:40
  352.8 5.8 %all-to-all-start.1 = ((bf16[4,32,384]{2,1,0:T(8,128)(2,1)}), bf16[4,32,384]{2,1,0:T(8,128)(2,1)S(1)}, u32[]{:S(2)}, u32[]{:S(2)}) async-start(bf16[4,32,384]{2,1,0:T(8,128)(2,1)} %bitcast.29), calls=%async_computation.6 | async-start | bytes 196608 | tf_op jit(solution)/shard_map/all_to_all | solution.py:41
  358.6 7.7 %fusion = bf16[384,3072]{0,1:T(8,128)(2,1)} fusion(bf16[1024,3072]{1,0:T(8,128)(2,1)} %all-gather.11.cloned.1.call-done, bf16[1024,384]{1,0:T(8,128)(2,1)S(1)} %all_gather.15), kind=kOutput, calls=%fused_computation.2 | convolution fusion | flops 2417098752 | bytes 9437184 | tf_op jit(solution)/shard_map/dot_general | solution.py:42
  366.3 4.3 copy.17
  370.6 0.7 copy.19
  371.3 65.5 %reduce-scatter.10.cloned.1.call-done = bf16[32,1536]{1,0:T(8,128)(2,1)} async-done(((bf16[1024,1536]{1,0:T(8,128)(2,1)}), bf16[32,1536]{1,0:T(8,128)(2,1)}) %reduce-scatter.10.cloned.1.call-update) | async-done | bytes 98320 | tf_op jit(solution)/shard_map/reduce_scatter | solution.py:33
  (19 shorter events, 0.5 us)
Async XLA Ops:
  8.0 40.4 %copy-start = (bf16[384,3072]{1,0:T(8,128)(2,1)S(1)}, bf16[384,3072]{1,0:T(8,128)(2,1)}, u32[]{:S(2)}) copy-start(bf16[384,3072]{1,0:T(8,128)(2,1)} %param.5) | copy-start | bytes 7077892
  8.0 54.9 %all-gather.7.cloned.1.call-start = ((), (), s32[]{:S(2)}) async-start(), calls=%async_computation.11 | async-start | bytes 3244032 | tf_op jit(solution)/shard_map/all_gather | solution.py:22
  8.7 114.9 %reduce-scatter.6.cloned.1.call-start = ((), (), s32[]{:S(2)}) async-start(), calls=%async_computation.7 | async-start | bytes 7864320 | tf_op jit(solution)/shard_map/reduce_scatter | solution.py:20
  53.8 98.2 %reduce-scatter.12.cloned.1.call-start = ((), (), s32[]{:S(2)}) async-start(), calls=%async_computation.12 | async-start | bytes 1966080 | tf_op jit(solution)/shard_map/reduce_scatter | solution.py:26
  69.3 110.3 %reduce-scatter.8.cloned.1.call-start = ((), (), s32[]{:S(2)}) async-start(), calls=%async_computation.8 | async-start | bytes 1966080 | tf_op jit(solution)/shard_map/reduce_scatter | solution.py:21
  123.7 84.0 %all-gather.9.cloned.1.call-start = ((), (), s32[]{:S(2)}) async-start(), calls=%async_computation.13 | async-start | bytes 1966080 | tf_op jit(solution)/shard_map/all_gather | solution.py:29
  182.1 93.2 %all-gather.11.cloned.1.call-start = ((), (), s32[]{:S(2)}) async-start(), calls=%async_computation.14 | async-start | bytes 7864320 | tf_op jit(solution)/shard_map/all_gather | solution.py:30
  207.7 96.3 %all-gather.5.cloned.1.call-start = ((), (), s32[]{:S(2)}) async-start(), calls=%async_computation.9 | async-start | bytes 1966080 | tf_op jit(solution)/shard_map/all_gather | solution.py:31
  208.5 144.3 %reduce-scatter.14.cloned.1.call-start = ((), (), s32[]{:S(2)}) async-start(), calls=%async_computation.15 | async-start | bytes 884736 | tf_op jit(solution)/shard_map/reduce_scatter | solution.py:40
  281.8 155.0 %reduce-scatter.10.cloned.1.call-start = ((), (), s32[]{:S(2)}) async-start(), calls=%async_computation.10 | async-start | bytes 3244032 | tf_op jit(solution)/shard_map/reduce_scatter | solution.py:33
  352.8 17.8 %all-to-all-start.1 = ((bf16[4,32,384]{2,1,0:T(8,128)(2,1)}), bf16[4,32,384]{2,1,0:T(8,128)(2,1)S(1)}, u32[]{:S(2)}, u32[]{:S(2)}) async-start(bf16[4,32,384]{2,1,0:T(8,128)(2,1)} %bitcast.29), calls=%async_computation.6 | async-start | bytes 196608 | tf_op jit(solution)/shard_map/all_to_all | solution.py:41
Sparse Core Ops, SparseCore 0:
  11.1 51.7 all-gather.6
  281.9 70.8 reduce-scatter.13
  357.0 79.7 reduce-scatter.9
Sparse Core Ops, SparseCore 1:
  53.9 69.7 reduce-scatter.5
  126.5 25.5 reduce-scatter.11
  154.4 25.2 reduce-scatter.7
  182.2 25.5 all-gather.8
  209.4 65.8 all-gather.10
  276.9 27.0 all-gather.4

commit v2 on v1

v2 whole, which is shorter than its diff:
```python
import jax
import jax.numpy as jnp
from jax import lax
from jax.experimental import pallas as pl
from jax.experimental.pallas import tpu as pltpu
from jax.sharding import PartitionSpec as P

BF16, F32 = jnp.bfloat16, jnp.float32
MESH = pl.DeviceIdType.MESH
NT = (((1,), (1,)), ((), ()))


def gelu_parts(pre):
    scaled = pre * 0.7071067811865476
    cdf = 0.5 * (1.0 + lax.erf(scaled))
    value = pre * cdf
    slope = cdf + pre * jnp.exp(-0.5 * pre * pre) * 0.3989422804014327
    return (value, slope)


MESSAGES = {}


def number(name, count):
    MESSAGES[name] = sum(size for _, size in LAYOUT[:[n for n, _ in LAYOUT].index(name)])
    return count


LAYOUT = [
    ("xz", 3), ("xx", 3), ("cz", 3), ("cx", 3), ("w1", 1), ("w2", 1),
    ("pa", 8), ("pb", 8), ("pc", 8), ("pz", 4),
    ("ga", 8), ("gb", 8), ("gc", 8),
    ("as", 8), ("af", 8), ("hz", 4), ("hs", 16), ("hf", 16),
    ("ox", 3), ("oz", 3), ("ix", 3), ("iz", 3), ("sg", 1), ("fg", 2),
]
for _name, _count in LAYOUT:
    number(_name, _count)
N_MESSAGES = sum(size for _, size in LAYOUT)


def kernel(
    x_ref, w1_ref, w2_ref, cot_ref,
    out_ref, ig_ref, fg_ref, sg_ref,
    w1, w2, xg, xgt, cotg,
    p, pa, pb, pc, ps, pr,
    g, ga, gb, gc,
    slope, act, actt, gh,
    o, orx, osum, orz, ofin,
    ig, irx, isum, irz, ifin,
    sgs, sgr, sgo, fgs, fgr, fgo,
    send_sem, recv_sem, local_sem,
):
    ia, y, al = lax.axis_index("ia"), lax.axis_index("ja"), lax.axis_index("al")
    x, z, zl, c = al // 2, lax.rem(al, 2) * 2 + ia // 2, ia // 2, lax.rem(ia, 2)

    def at_x(d):
        return (ia, y, lax.rem(x + d + 4, 4) * 2 + lax.rem(al, 2))

    def at_y(d):
        return (ia, lax.rem(y + d + 4, 4), al)

    def at_z(d):
        other = lax.rem(z + d + 4, 4)
        return (lax.rem(other, 2) * 2 + c, y, x * 2 + other // 2)

    core = (zl * 2 + 1 - c, y, al)
    pair = ((1 - zl) * 2 + c, y, al)
    y1, y2, y3 = lax.rem(y + 1, 4), lax.rem(y + 2, 4), lax.rem(y + 3, 4)

    barrier = pltpu.get_barrier_semaphore()
    partners = [at_x(1), at_x(2), at_x(3), at_y(1), at_y(3), at_z(1), at_z(2), at_z(3), core]
    for partner in partners:
        pl.semaphore_signal(barrier, inc=1, device_id=partner, device_id_type=MESH)

    sent = {}

    def copy(name, k, src, dst, device):
        i = MESSAGES[name] + k
        made = pltpu.make_async_remote_copy(
            src_ref=src, dst_ref=dst, send_sem=send_sem.at[i], recv_sem=recv_sem.at[i],
            device_id=device, device_id_type=MESH,
        )
        made.start()
        sent[(name, k)] = made

    def arrived(name, k):
        sent[(name, k)].wait_recv()

    n_local = [0]

    def local(src, dst):
        made = pltpu.make_async_copy(src, dst, local_sem.at[n_local[0]])
        made.start()
        n_local[0] += 1
        return made

    own_half = pl.ds(pl.multiple_of(zl * 768, 768), 768)
    other_half = pl.ds(pl.multiple_of((1 - zl) * 768, 768), 768)
    w1_rows = pl.ds(pl.multiple_of(c * 384, 384), 384)
    w2_rows = pl.ds(pl.multiple_of(c * 768, 768), 768)
    load_x = local(x_ref.at[:, own_half], xg.at[0, z])
    load_w1 = local(w1_ref, w1.at[w1_rows])
    load_cot = local(cot_ref, cotg.at[0, z])
    load_w2 = local(w2_ref, w2.at[w2_rows])

    pl.semaphore_wait(barrier, len(partners))

    copy("xz", 0, x_ref.at[:, other_half], xg.at[0, z], at_z(1))
    copy("xz", 2, x_ref.at[:, other_half], xg.at[0, z], at_z(3))
    copy("xz", 1, x_ref.at[:, own_half], xg.at[0, z], at_z(2))
    copy("w1", 0, w1_ref, w1.at[w1_rows], core)
    for d in (1, 3, 2):
        copy("cz", d - 1, cot_ref, cotg.at[0, z], at_z(d))
    copy("w2", 0, w2_ref, w2.at[w2_rows], core)

    load_x.wait()
    for k in range(3):
        arrived("xz", k)
    for d in (1, 3, 2):
        copy("xx", d - 1, xg.at[0], xg.at[4 - d], at_x(d))
    load_w1.wait()
    arrived("w1", 0)

    def rows(block, half):
        return pl.ds(pl.multiple_of(block * 32 + half * 16, 16), 16)

    def pre_product(r):
        lhs = xg[r].reshape(128, 768)

        @pl.loop(0, 4)
        def _(t):
            cols = pl.ds(pl.multiple_of(t * 768, 768), 768)
            inner = pl.ds(pl.multiple_of(lax.rem(t, 2) * 768, 768), 768)
            p[r, t // 2, :, inner] = jnp.dot(lhs, w1[:, cols], preferred_element_type=F32).astype(BF16)

        copy("pa", 2 * r, p.at[r, :, rows(y2, 0)], pa.at[r, 0], at_y(3))
        copy("pa", 2 * r + 1, p.at[r, :, rows(y2, 1)], pa.at[r, 1], at_y(1))
        copy("pb", 2 * r, p.at[r, :, rows(y3, 1)], pb.at[r, 0], at_y(3))
        copy("pb", 2 * r + 1, p.at[r, :, rows(y1, 0)], pb.at[r, 1], at_y(1))

    def pre_forward(r):
        for side, (block, half, device) in enumerate(((y3, 0, at_y(3)), (y1, 1, at_y(1)))):
            arrived("pa", 2 * r + side)
            spot = rows(block, half)
            p[r, :, spot] = (p[r, :, spot].astype(F32) + pa[r, side].astype(F32)).astype(BF16)
            copy("pc", 2 * r + side, p.at[r, :, spot], pc.at[r, side], device)

    def pre_block(r, hidden):
        low = p[r, hidden, rows(y, 0)].astype(F32) + pb[r, 1, hidden].astype(F32) + pc[r, 0, hidden].astype(F32)
        high = p[r, hidden, rows(y, 1)].astype(F32) + pb[r, 0, hidden].astype(F32) + pc[r, 1, hidden].astype(F32)
        return jnp.concatenate([low, high], axis=0)

    def pre_sum(r):
        for side in range(2):
            arrived("pb", 2 * r + side)
            arrived("pc", 2 * r + side)
        ps[r] = pre_block(r, 1 - zl).astype(BF16)
        copy("pz", r, ps.at[r], pr.at[r], pair)

    def act_send(r):
        own = act.at[r, y]
        copy("as", 2 * r, own, own, at_y(3))
        copy("as", 2 * r + 1, own, own, at_y(1))

    def gelu(r):
        arrived("pz", r)
        value, slope[r] = gelu_parts(pre_block(r, zl) + pr[r].astype(F32))
        act[r, y] = value.astype(BF16)
        act_send(r)

    def act_forward(r):
        arrived("as", 2 * r)
        low = act.at[r, y1, pl.ds(0, 16)]
        copy("af", 2 * r, low, low, at_y(3))
        arrived("as", 2 * r + 1)
        high = act.at[r, y3, pl.ds(16, 16)]
        copy("af", 2 * r + 1, high, high, at_y(1))

    def grad_product(r):
        lhs = cotg[r].reshape(128, 1536)

        @pl.loop(0, 3)
        def _(t):
            cols = pl.ds(pl.multiple_of(t * 512, 512), 512)
            g[r, :, cols] = lax.dot_general(lhs, w2[cols, :], NT, preferred_element_type=F32).astype(BF16)

        copy("ga", 2 * r, g.at[r, rows(y2, 0)], ga.at[r, 0], at_y(3))
        copy("ga", 2 * r + 1, g.at[r, rows(y2, 1)], ga.at[r, 1], at_y(1))
        copy("gb", 2 * r, g.at[r, rows(y3, 1)], gb.at[r, 0], at_y(3))
        copy("gb", 2 * r + 1, g.at[r, rows(y1, 0)], gb.at[r, 1], at_y(1))

    def grad_forward(r):
        for side, (block, half, device) in enumerate(((y3, 0, at_y(3)), (y1, 1, at_y(1)))):
            arrived("ga", 2 * r + side)
            spot = rows(block, half)
            g[r, spot] = (g[r, spot].astype(F32) + ga[r, side].astype(F32)).astype(BF16)
            copy("gc", 2 * r + side, g.at[r, spot], gc.at[r, side], device)

    def hid_send(r, hidden, which):
        own = gh.at[r, hidden, y]
        copy("hs", 4 * r + 2 * which, own, own, at_y(3))
        copy("hs", 4 * r + 2 * which + 1, own, own, at_y(1))

    def hidden_grad(r):
        for side in range(2):
            arrived("gb", 2 * r + side)
            arrived("gc", 2 * r + side)
        low = g[r, rows(y, 0)].astype(F32) + gb[r, 1].astype(F32) + gc[r, 0].astype(F32)
        high = g[r, rows(y, 1)].astype(F32) + gb[r, 0].astype(F32) + gc[r, 1].astype(F32)
        gh[r, zl, y] = (jnp.concatenate([low, high], axis=0) * slope[r]).astype(BF16)
        own = gh.at[r, zl, y]
        copy("hz", r, own, own, pair)
        hid_send(r, zl, 0)

    def hidden_pair(r):
        arrived("hz", r)
        hid_send(r, 1 - zl, 1)

    def hid_forward(r, which):
        hidden = zl if which == 0 else 1 - zl
        k = 4 * r + 2 * which
        arrived("hs", k)
        low = gh.at[r, hidden, y1, pl.ds(0, 16)]
        copy("hf", k, low, low, at_y(3))
        arrived("hs", k + 1)
        high = gh.at[r, hidden, y3, pl.ds(16, 16)]
        copy("hf", k + 1, high, high, at_y(1))

    def out_product(r):
        arrived("af", 2 * r)
        arrived("af", 2 * r + 1)
        lhs = act[r].reshape(128, 1536)

        @pl.loop(0, 3)
        def _(t):
            cols = pl.ds(pl.multiple_of(t * 512, 512), 512)
            o[r, :, cols] = jnp.dot(lhs, w2[:, cols], preferred_element_type=F32).astype(BF16)

        if r:
            copy("ox", r - 1, o.at[r], orx.at[r - 1], at_x(r))

    def out_sum():
        for r in range(1, 4):
            arrived("ox", r - 1)
        total = o[0].astype(F32) + orx[0].astype(F32) + orx[1].astype(F32) + orx[2].astype(F32)
        osum[...] = total.astype(BF16).reshape(4, 32, 1536)
        for d in range(1, 4):
            copy("oz", d - 1, osum.at[lax.rem(z + d, 4)], orz.at[d - 1], at_z(d))

    def out_final():
        for d in range(1, 4):
            arrived("oz", d - 1)
        total = osum[z].astype(F32) + orz[0].astype(F32) + orz[1].astype(F32) + orz[2].astype(F32)
        ofin[...] = total.astype(BF16)
        return local(ofin, out_ref)

    def second_grad():
        for r in range(4):
            actt[:, pl.ds(r * 128, 128)] = act[r].reshape(128, 1536).T
        rhs = cotg[...].reshape(512, 1536)
        base = (1 - c) * 768

        @pl.loop(0, 3)
        def _(t):
            some = pl.ds(pl.multiple_of(base + t * 256, 256), 256)
            sgs[pl.ds(pl.multiple_of(t * 256, 256), 256)] = jnp.dot(
                actt[some], rhs, preferred_element_type=F32
            ).astype(BF16)

        copy("sg", 0, sgs, sgr, core)

    def second_grad_own():
        arrived("sg", 0)
        rhs = cotg[...].reshape(512, 1536)

        @pl.loop(0, 3)
        def _(t):
            some = pl.ds(pl.multiple_of(c * 768 + t * 256, 256), 256)
            inner = pl.ds(pl.multiple_of(t * 256, 256), 256)
            total = jnp.dot(actt[some], rhs, preferred_element_type=F32) + sgr[inner].astype(F32)
            sgo[inner] = total.astype(BF16)

        return local(sgo, sg_ref)

    def in_product(r):
        for k in range(4):
            arrived("hf", 4 * r + k)
        first = gh[r, 0].reshape(128, 1536)
        second = gh[r, 1].reshape(128, 1536)

        @pl.loop(0, 3)
        def _(t):
            some = pl.ds(pl.multiple_of(t * 256, 256), 256)
            total = lax.dot_general(first, w1[some, pl.ds(0, 1536)], NT, preferred_element_type=F32)
            total += lax.dot_general(second, w1[some, pl.ds(1536, 1536)], NT, preferred_element_type=F32)
            ig[r, :, some] = total.astype(BF16)

        if r:
            copy("ix", r - 1, ig.at[r], irx.at[r - 1], at_x(r))

    def in_sum():
        for r in range(1, 4):
            arrived("ix", r - 1)
        total = ig[0].astype(F32) + irx[0].astype(F32) + irx[1].astype(F32) + irx[2].astype(F32)
        isum[...] = total.astype(BF16).reshape(4, 32, 768)
        for d in range(1, 4):
            copy("iz", d - 1, isum.at[lax.rem(z + d, 4)], irz.at[d - 1], at_z(d))

    def in_final():
        for d in range(1, 4):
            arrived("iz", d - 1)
        ifin[0] = (isum[z].astype(F32) + irz[1].astype(F32)).astype(BF16)
        ifin[1] = (irz[0].astype(F32) + irz[2].astype(F32)).astype(BF16)
        return [local(ifin.at[0], ig_ref.at[:, own_half]), local(ifin.at[1], ig_ref.at[:, other_half])]

    def transpose_in():
        for r in range(4):
            xgt[:, pl.ds(r * 128, 128)] = xg[r].reshape(128, 768).T

    def first_grad(half):
        lhs = xgt[pl.ds(pl.multiple_of((1 - c) * 384, 128), 384)]
        rhs = gh.at[:, half]

        @pl.loop(0, 3)
        def _(t):
            cols = pl.ds(pl.multiple_of(t * 512, 512), 512)
            some = gh[:, half, :, :, cols].reshape(512, 512)
            fgs[half, :, cols] = jnp.dot(lhs, some, preferred_element_type=F32).astype(BF16)

        copy("fg", half, fgs.at[half], fgr.at[half], core)

    def first_grad_own(half):
        arrived("fg", half)
        lhs = xgt[pl.ds(pl.multiple_of(c * 384, 128), 384)]

        @pl.loop(0, 3)
        def _(t):
            cols = pl.ds(pl.multiple_of(t * 512, 512), 512)
            some = gh[:, half, :, :, cols].reshape(512, 512)
            total = jnp.dot(lhs, some, preferred_element_type=F32) + fgr[half, :, cols].astype(F32)
            fgo[half, :, cols] = total.astype(BF16)

        return local(fgo.at[half], fg_ref.at[:, pl.ds(half * 1536, 1536)])

    pre_product(0)
    load_cot.wait()
    for k in range(3):
        arrived("cz", k)
    for d in (1, 3, 2):
        copy("cx", d - 1, cotg.at[0], cotg.at[4 - d], at_x(d))
    load_w2.wait()
    arrived("w2", 0)
    arrived("xx", 2)
    pre_product(1)
    pre_forward(0)
    arrived("xx", 0)
    pre_product(3)
    pre_forward(1)
    arrived("xx", 1)
    pre_product(2)
    pre_forward(3)
    pre_sum(0)
    transpose_in()
    pre_forward(2)
    arrived("cx", 2)
    grad_product(1)
    pre_sum(1)
    arrived("cx", 0)
    grad_product(3)
    gelu(0)
    pre_sum(3)
    grad_forward(1)
    arrived("cx", 1)
    grad_product(2)
    gelu(1)
    pre_sum(2)
    grad_forward(3)
    grad_product(0)
    gelu(3)
    hidden_grad(1)
    grad_forward(2)
    act_forward(0)
    gelu(2)
    hidden_grad(3)
    grad_forward(0)
    act_forward(1)
    hidden_pair(1)
    hidden_pair(3)
    hidden_grad(2)
    act_forward(3)
    hid_forward(1, 0)
    hidden_grad(0)
    act_forward(2)
    hidden_pair(2)
    out_product(1)
    hid_forward(3, 0)
    hidden_pair(0)
    out_product(3)
    hid_forward(1, 1)
    hid_forward(3, 1)
    out_product(2)
    hid_forward(2, 0)
    out_product(0)
    in_product(1)
    hid_forward(0, 0)
    out_sum()
    in_product(3)
    hid_forward(2, 1)
    second_grad()
    hid_forward(0, 1)
    done = [out_final()]
    done.append(second_grad_own())
    in_product(2)
    in_product(0)
    in_sum()
    first_grad(0)
    first_grad(1)
    done += in_final()
    done.append(first_grad_own(0))
    done.append(first_grad_own(1))
    for made in sent.values():
        made.wait_send()
    for made in done:
        made.wait()


def shards(inputs, first_weight, second_weight, cotangent):
    def vmem(*shape, dtype=BF16):
        return pltpu.VMEM(shape, dtype)

    anywhere = pl.BlockSpec(memory_space=pl.ANY)
    return pl.pallas_call(
        kernel,
        out_shape=[
            jax.ShapeDtypeStruct((32, 1536), BF16),
            jax.ShapeDtypeStruct((32, 1536), BF16),
            jax.ShapeDtypeStruct((384, 3072), BF16),
            jax.ShapeDtypeStruct((768, 1536), BF16),
        ],
        in_specs=[anywhere] * 4,
        out_specs=[anywhere] * 4,
        scratch_shapes=[
            vmem(768, 3072), vmem(1536, 1536), vmem(4, 4, 32, 768), vmem(768, 512), vmem(4, 4, 32, 1536),
            vmem(4, 2, 128, 1536), vmem(4, 2, 2, 16, 1536), vmem(4, 2, 2, 16, 1536), vmem(4, 2, 2, 16, 1536),
            vmem(4, 32, 1536), vmem(4, 32, 1536),
            vmem(4, 128, 1536), vmem(4, 2, 16, 1536), vmem(4, 2, 16, 1536), vmem(4, 2, 16, 1536),
            vmem(4, 32, 1536, dtype=F32), vmem(4, 4, 32, 1536), vmem(1536, 512), vmem(4, 2, 4, 32, 1536),
            vmem(4, 128, 1536), vmem(3, 128, 1536), vmem(4, 32, 1536), vmem(3, 32, 1536), vmem(32, 1536),
            vmem(4, 128, 768), vmem(3, 128, 768), vmem(4, 32, 768), vmem(3, 32, 768), vmem(2, 32, 768),
            vmem(768, 1536), vmem(768, 1536), vmem(768, 1536),
            vmem(2, 384, 1536), vmem(2, 384, 1536), vmem(2, 384, 1536),
            pltpu.SemaphoreType.DMA((N_MESSAGES,)),
            pltpu.SemaphoreType.DMA((N_MESSAGES,)),
            pltpu.SemaphoreType.DMA((10,)),
        ],
        compiler_params=pltpu.CompilerParams(
            collective_id=0, has_side_effects=True, vmem_limit_bytes=60 << 20
        ),
        name="layer",
    )(inputs, first_weight, second_weight, cotangent)


def solution(mesh):
    in_specs = (
        P(("ia", "al"), "ja"),
        P(("ja", "ia"), "al"),
        P(("al", "ia"), "ja"),
        P(("ia", "al"), "ja"),
    )
    out_specs = (
        P(("ia", "al"), "ja"),
        P(("ia", "al"), "ja"),
        P(("ja", "ia"), "al"),
        P(("al", "ia"), "ja"),
    )
    return jax.shard_map(shards, mesh=mesh, in_specs=in_specs, out_specs=out_specs, check_vma=False)
```

time: 445 us -> 132 us (0.30)
  waiting for transfers between devices: 337 us -> 0 us
  Pallas kernels: 0 us -> 121 us
  matrix products: 38.8 us -> 0 us
  blocking collectives: 38.7 us -> 0 us
  between operations: 15.3 us -> 0.64 us
  starting transfers between devices: 6.19 us -> 0 us
    reduce_scatter x5 -> x0, waiting for transfers between devices: 212 us -> none  [the longest x1 65.5 us: shards(): lax.psum_scatter(output, ('al', 'ia'), scatter_dimension=0, tiled=True)]
    all_gather x4 -> x0, waiting for transfers between devices: 124 us -> none  [the longest x1 66.7 us: shards(): grad_hid = lax.all_gather(grad_hid, 'ja', axis=0, tiled=True)]
    pallas_call x0 -> x1, Pallas kernels: none -> 121 us  [shards(): pl.pallas_call(kernel, out_shape=[jax.ShapeDtypeStruct((32, 1536), BF16),...]
    dot_general x6 -> x0, matrix products: 38.8 us -> none  [the longest x1 7.72 us: shards(): lax.dot_general(tokens, grad_hid, (((0,), (0,)), ((), ())), preferred_ele...]
    all_gather x1 -> x0, blocking collectives: 30.9 us -> none  [shards(): tokens = lax.all_gather(mine, 'al', axis=0, tiled=True)]
    all_to_all x1 -> x0, blocking collectives: 7.84 us -> none  [shards(): mine = lax.all_to_all(inputs, 'ia', split_axis=1, concat_axis=0, tiled=True)]
    all_to_all x1 -> x0, starting transfers between devices: 5.81 us -> none  [shards(): lax.all_to_all(input_grad, 'ia', split_axis=0, concat_axis=1, tiled=True)]
  transfers between devices with their start and end apart: 10 -> 0, of which waited for: 9 -> 0; matrix products, arithmetic and copies ran while one was open for 10% -> 0% of each run, Pallas kernels for 0% -> 0%
where the time goes in v2:
time: 132 us; the launch traced here: 130 us
  Pallas kernels  121 us (92%)
  local copies, waits for them, and re-layouts  7.86 us (6%)
    pallas_call x1, Pallas kernels, shards(): pl.pallas_call(kernel, out_shape=[jax.ShapeDtypeStruct((32, 1536), BF16),...  121 us
    unnamed x6, local copies, waits for them, and re-layouts  7.86 us

profile of v2, /device:TPU:1, one launch (start us, length us, event | category | flops | bytes accessed | tf_op | source)
XLA Modules:
  0.0 129.8 jit_solution(818542655258144784)
XLA Ops:
  0.6 121.3 %layer.1 = (bf16[32,1536]{1,0:T(8,128)(2,1)}, bf16[32,1536]{1,0:T(8,128)(2,1)}, bf16[384,3072]{1,0:T(8,128)(2,1)}, bf16[768,1536]{1,0:T(8,128)(2,1)}) custom-call(bf16[32,1536]{1,0:T(8,128)(2,1)} %x_ref.1, bf16[384,3072]{1,0:T(8,128)(2,1)} %w1_ref.1, bf16[768,1536]{1,0:T(8,128)(2,1)} %w2_ref.1, bf16[32,1536]{1,0:T(8,128)(2,1)} %cot_ref.1), custom_call_target="tpu_custom_call" | custom-call | tf_op jit(solution)/shard_map/layer/pallas_call | solution.py:432
  122.0 1.5 %copy.12 = bf16[32,1536]{1,0:T(8,128)(2,1)} copy(bf16[32,1536]{1,0:T(8,128)(2,1)} %get-tuple-element.8) | data formatting | bytes 196608
  123.5 1.5 %copy.13 = bf16[32,1536]{1,0:T(8,128)(2,1)} copy(bf16[32,1536]{1,0:T(8,128)(2,1)} %get-tuple-element.9) | data formatting | bytes 196608
  125.0 0.0 copy-start
  125.0 3.4 %copy.14 = bf16[384,3072]{1,0:T(8,128)(2,1)} copy(bf16[384,3072]{1,0:T(8,128)(2,1)} %get-tuple-element.10) | data formatting | bytes 4718592
  128.4 0.0 copy-done
  128.4 1.4 %copy.15 = bf16[768,1536]{1,0:T(8,128)(2,1)} copy(bf16[768,1536]{1,0:T(8,128)(2,1)S(1)} %copy-done) | data formatting | bytes 4718592
Async XLA Ops:
  125.0 3.4 %copy-start = (bf16[768,1536]{1,0:T(8,128)(2,1)S(1)}, bf16[768,1536]{1,0:T(8,128)(2,1)}, u32[]{:S(2)}) copy-start(bf16[768,1536]{1,0:T(8,128)(2,1)} %get-tuple-element.11) | copy-start | bytes 7077892

commit v3 on v2

v3 whole, which is shorter than its diff:
```python
import jax
import jax.numpy as jnp
from jax import lax
from jax.experimental import pallas as pl
from jax.experimental.pallas import tpu as pltpu
from jax.sharding import PartitionSpec as P

BF16, F32 = jnp.bfloat16, jnp.float32
MESH = pl.DeviceIdType.MESH

OFFSET = (0, 2, 1, 3)
SLOT = {offset: slot for slot, offset in enumerate(OFFSET)}
PRE_CROSS = (2,)
HID_CROSS = (2, 3)


def gelu_parts(pre):
    scaled = pre * 0.7071067811865476
    cdf = 0.5 * (1.0 + lax.erf(scaled))
    value = pre * cdf
    slope = cdf + pre * jnp.exp(-0.5 * pre * pre) * 0.3989422804014327
    return (value, slope)


MESSAGES = {}


def number(name, count):
    MESSAGES[name] = sum(size for _, size in LAYOUT[:[n for n, _ in LAYOUT].index(name)])
    return count


LAYOUT = [
    ("xz", 3), ("xx", 2), ("xf", 2), ("cz", 3), ("cx", 2), ("cf", 2), ("w1", 1), ("w2", 1),
    ("pa", 8), ("pb", 8), ("pc", 8), ("pz", 4),
    ("ga", 8), ("gb", 8), ("gc", 8),
    ("as", 8), ("af", 8), ("hz", 20), ("hs", 16), ("hf", 16),
    ("ox", 3), ("oz", 3), ("ix", 3), ("iz", 3), ("sg", 1), ("fg", 2),
]
for _name, _count in LAYOUT:
    number(_name, _count)
N_MESSAGES = sum(size for _, size in LAYOUT)


def kernel(
    x_ref, w1_ref, w2_ref, cot_ref,
    out_ref, ig_ref, fg_ref, sg_ref,
    w1, w2, wt, xg, xgt, cotg,
    p, pa, pb, pc, ps, pr, prc,
    g, ga, gb, gc,
    slope, act, actt, gh,
    orx, osum, orz,
    ig, irx, isum, irz,
    gone, sgr, fgr,
    send_sem, recv_sem, local_sem,
):
    ia, y, al = lax.axis_index("ia"), lax.axis_index("ja"), lax.axis_index("al")
    x, z, zl, c = al // 2, lax.rem(al, 2) * 2 + ia // 2, ia // 2, lax.rem(ia, 2)

    def at_x(d):
        return (ia, y, lax.rem(x + d + 4, 4) * 2 + lax.rem(al, 2))

    def at_y(d):
        return (ia, lax.rem(y + d + 4, 4), al)

    def at_z(d):
        other = lax.rem(z + d + 4, 4)
        return (lax.rem(other, 2) * 2 + c, y, x * 2 + other // 2)

    core = (zl * 2 + 1 - c, y, al)
    pair = ((1 - zl) * 2 + c, y, al)
    y1, y2, y3 = lax.rem(y + 1, 4), lax.rem(y + 2, 4), lax.rem(y + 3, 4)

    barrier = pltpu.get_barrier_semaphore()
    partners = [at_x(1), at_x(2), at_x(3), at_y(1), at_y(3), at_z(1), at_z(2), at_z(3), core]
    for partner in partners:
        pl.semaphore_signal(barrier, inc=1, device_id=partner, device_id_type=MESH)

    sent = {}

    def copy(name, k, src, dst, device):
        i = MESSAGES[name] + k
        made = pltpu.make_async_remote_copy(
            src_ref=src, dst_ref=dst, send_sem=send_sem.at[i], recv_sem=recv_sem.at[i],
            device_id=device, device_id_type=MESH,
        )
        made.start()
        sent[(name, k)] = made

    def left(name, k):
        sent.pop((name, k)).wait_send()

    def arrived(name, k):
        sent[(name, k)].wait_recv()

    n_local = [0]

    def local(src, dst):
        made = pltpu.make_async_copy(src, dst, local_sem.at[n_local[0]])
        made.start()
        n_local[0] += 1
        return made

    own_half = pl.ds(pl.multiple_of(zl * 768, 768), 768)
    other_half = pl.ds(pl.multiple_of((1 - zl) * 768, 768), 768)
    w1_rows = pl.ds(pl.multiple_of(c * 384, 384), 384)
    w2_rows = pl.ds(pl.multiple_of(c * 768, 768), 768)
    load_x = local(x_ref.at[:, own_half], xg.at[0, z])
    load_w1 = local(w1_ref, w1.at[w1_rows])
    load_cot = local(cot_ref, cotg.at[0, z])
    load_w2 = local(w2_ref, w2.at[w2_rows])

    pl.semaphore_wait(barrier, len(partners))

    copy("xz", 0, x_ref.at[:, other_half], xg.at[0, z], at_z(1))
    copy("xz", 2, x_ref.at[:, other_half], xg.at[0, z], at_z(3))
    copy("xz", 1, x_ref.at[:, own_half], xg.at[0, z], at_z(2))
    copy("w1", 0, w1_ref, w1.at[w1_rows], core)
    for d in (1, 3, 2):
        copy("cz", d - 1, cot_ref, cotg.at[0, z], at_z(d))
    copy("w2", 0, w2_ref, w2.at[w2_rows], core)

    def spread(name, buffer):
        copy(name, 0, buffer.at[0], buffer.at[SLOT[1]], at_x(3))
        copy(name, 1, buffer.at[0], buffer.at[SLOT[3]], at_x(1))

    def pass_on(name, far, buffer, side):
        arrived(name, side)
        slot, half, device = ((SLOT[1], 0, at_x(3)), (SLOT[3], 2, at_x(1)))[side]
        part = pl.ds(half, 2)
        copy(far, side, buffer.at[slot, part], buffer.at[SLOT[2], part], device)

    load_x.wait()
    for k in range(3):
        arrived("xz", k)
    spread("xx", xg)
    load_w1.wait()
    arrived("w1", 0)

    def rows(block, half):
        return pl.ds(pl.multiple_of(block * 32 + half * 16, 16), 16)

    def pre_product(r):
        lhs = xg[r].reshape(128, 768)

        for half in range(2):
            cols = pl.ds(half * 1536, 1536)
            p[r, half] = jnp.dot(lhs, w1[:, cols], preferred_element_type=F32).astype(BF16)

        if r in PRE_CROSS:
            copy("pz", r, p.at[r, 1 - zl], prc.at[PRE_CROSS.index(r)], pair)
        else:
            pre_send(r)

    def pre_view(r):
        return p.at[r, pl.ds(zl, 1)] if r in PRE_CROSS else p.at[r]

    def pre_room(buffer, r, side):
        return buffer.at[r, side, pl.ds(0, 1)] if r in PRE_CROSS else buffer.at[r, side]

    def pre_send(r):
        mine = pre_view(r)
        copy("pa", 2 * r, mine.at[:, rows(y2, 0)], pre_room(pa, r, 0), at_y(3))
        copy("pa", 2 * r + 1, mine.at[:, rows(y2, 1)], pre_room(pa, r, 1), at_y(1))
        copy("pb", 2 * r, mine.at[:, rows(y3, 1)], pre_room(pb, r, 0), at_y(3))
        copy("pb", 2 * r + 1, mine.at[:, rows(y1, 0)], pre_room(pb, r, 1), at_y(1))

    def pre_cross(r):
        arrived("pz", r)

        @pl.loop(0, 4)
        def _(t):
            some = pl.ds(pl.multiple_of(t * 32, 32), 32)
            p[r, zl, some] = (p[r, zl, some].astype(F32) + prc[PRE_CROSS.index(r), some].astype(F32)).astype(BF16)

        pre_send(r)

    def pre_forward(r):
        mine = pre_view(r)
        for side, (block, half, device) in enumerate(((y3, 0, at_y(3)), (y1, 1, at_y(1)))):
            arrived("pa", 2 * r + side)
            spot = rows(block, half)
            mine[:, spot] = (mine[:, spot].astype(F32) + pre_room(pa, r, side)[...].astype(F32)).astype(BF16)
            copy("pc", 2 * r + side, mine.at[:, spot], pre_room(pc, r, side), device)

    def pre_block(r, hidden):
        k = 0 if r in PRE_CROSS else hidden
        low = p[r, hidden, rows(y, 0)].astype(F32) + pb[r, 1, k].astype(F32) + pc[r, 0, k].astype(F32)
        high = p[r, hidden, rows(y, 1)].astype(F32) + pb[r, 0, k].astype(F32) + pc[r, 1, k].astype(F32)
        return jnp.concatenate([low, high], axis=0)

    def pre_sum(r):
        for side in range(2):
            arrived("pb", 2 * r + side)
            arrived("pc", 2 * r + side)
        if r not in PRE_CROSS:
            ps[r] = pre_block(r, 1 - zl).astype(BF16)
            copy("pz", r, ps.at[r], pr.at[r], pair)

    def act_send(r):
        own = act.at[r, y]
        copy("as", 2 * r, own, own, at_y(3))
        copy("as", 2 * r + 1, own, own, at_y(1))

    def gelu(r):
        pre = pre_block(r, zl)
        if r not in PRE_CROSS:
            arrived("pz", r)
            pre += pr[r].astype(F32)
        value, slope[r] = gelu_parts(pre)
        act[r, y] = value.astype(BF16)

    def act_forward(r):
        arrived("as", 2 * r)
        low = act.at[r, y1, pl.ds(0, 16)]
        copy("af", 2 * r, low, low, at_y(3))
        arrived("as", 2 * r + 1)
        high = act.at[r, y3, pl.ds(16, 16)]
        copy("af", 2 * r + 1, high, high, at_y(1))

    def grad_product(r):
        lhs = cotg[r].reshape(128, 1536)
        for half in range(2):
            cols = pl.ds(half * 768, 768)
            g[r, :, cols] = jnp.dot(lhs, wt[half], preferred_element_type=F32).astype(BF16)

        copy("ga", 2 * r, g.at[r, rows(y2, 0)], ga.at[r, 0], at_y(3))
        copy("ga", 2 * r + 1, g.at[r, rows(y2, 1)], ga.at[r, 1], at_y(1))
        copy("gb", 2 * r, g.at[r, rows(y3, 1)], gb.at[r, 0], at_y(3))
        copy("gb", 2 * r + 1, g.at[r, rows(y1, 0)], gb.at[r, 1], at_y(1))

    def grad_forward(r):
        for side, (block, half, device) in enumerate(((y3, 0, at_y(3)), (y1, 1, at_y(1)))):
            arrived("ga", 2 * r + side)
            spot = rows(block, half)
            g[r, spot] = (g[r, spot].astype(F32) + ga[r, side].astype(F32)).astype(BF16)
            copy("gc", 2 * r + side, g.at[r, spot], gc.at[r, side], device)

    def hid_send(r, hidden, which):
        own = gh.at[r, hidden, y]
        copy("hs", 4 * r + 2 * which, own, own, at_y(3))
        copy("hs", 4 * r + 2 * which + 1, own, own, at_y(1))

    def hidden_grad(r):
        for side in range(2):
            arrived("gb", 2 * r + side)
            arrived("gc", 2 * r + side)
        low = g[r, rows(y, 0)].astype(F32) + gb[r, 1].astype(F32) + gc[r, 0].astype(F32)
        high = g[r, rows(y, 1)].astype(F32) + gb[r, 0].astype(F32) + gc[r, 1].astype(F32)
        gh[r, zl, y] = (jnp.concatenate([low, high], axis=0) * slope[r]).astype(BF16)
        own = gh.at[r, zl, y]
        hid_pair_send(r, 0, own)
        hid_send(r, zl, 0)

    def hid_pair_send(r, k, part):
        copy("hz", 5 * r + k, part, part, pair)

    def hidden_pair(r):
        arrived("hz", 5 * r)
        hid_send(r, 1 - zl, 1)

    def hid_rest(r):
        arrived("hf", 4 * r)
        hid_pair_send(r, 3, gh.at[r, zl, y2, pl.ds(0, 16)])
        arrived("hf", 4 * r + 1)
        hid_pair_send(r, 4, gh.at[r, zl, y2, pl.ds(16, 16)])

    def hid_forward(r, which):
        hidden = zl if which == 0 else 1 - zl
        k = 4 * r + 2 * which
        arrived("hs", k)
        low = gh.at[r, hidden, y1, pl.ds(0, 16)]
        copy("hf", k, low, low, at_y(3))
        arrived("hs", k + 1)
        high = gh.at[r, hidden, y3, pl.ds(16, 16)]
        copy("hf", k + 1, high, high, at_y(1))
        if r in HID_CROSS:
            hid_pair_send(r, 1, gh.at[r, hidden, y1])
            hid_pair_send(r, 2, gh.at[r, hidden, y3])

    def out_product(r):
        arrived("af", 2 * r)
        arrived("af", 2 * r + 1)
        for name in ("ga", "gb", "gc"):
            for side in range(2):
                left(name, 2 * r + side)
        lhs = act[r].reshape(128, 1536)
        g[r] = jnp.dot(lhs, w2[...], preferred_element_type=F32).astype(BF16)
        if r:
            copy("ox", r - 1, g.at[r], orx.at[r - 1], at_x(OFFSET[r]))

    def out_sum():
        for r in range(1, 4):
            arrived("ox", r - 1)
        total = g[0].astype(F32) + orx[0].astype(F32) + orx[1].astype(F32) + orx[2].astype(F32)
        osum[...] = total.astype(BF16).reshape(4, 32, 1536)
        for d in range(1, 4):
            copy("oz", d - 1, osum.at[lax.rem(z + d, 4)], orz.at[d - 1], at_z(d))

    def out_final():
        for d in range(1, 4):
            arrived("oz", d - 1)
        total = osum[z].astype(F32) + orz[0].astype(F32) + orz[1].astype(F32) + orz[2].astype(F32)
        out_ref[...] = total.astype(BF16)

    def second_part(whose):
        core_rows = pl.ds(pl.multiple_of((c if whose else 1 - c) * 768, 256), 768)
        lhs = actt[core_rows]
        for t in range(3):
            cols = pl.ds(t * 512, 512)
            rhs = cotg[:, :, :, cols].reshape(512, 512)
            total = jnp.dot(lhs, rhs, preferred_element_type=F32)
            if whose:
                sg_ref[:, cols] = (total + sgr[:, :, cols].reshape(768, 512).astype(F32)).astype(BF16)
            else:
                for part in range(2):
                    gone[part, :, cols] = total[part * 384 : part * 384 + 384].astype(BF16)

    def second_grad():
        for r in range(4):
            actt[:, pl.ds(r * 128, 128)] = act[r].reshape(128, 1536).T
        second_part(0)
        copy("sg", 0, gone, sgr, core)

    def second_grad_own():
        arrived("sg", 0)
        second_part(1)
        left("sg", 0)

    def in_product(r):
        if r in HID_CROSS:
            for k in range(5):
                arrived("hz", 5 * r + k)
        else:
            for k in range(4):
                arrived("hf", 4 * r + k)
        first = gh[r, 0].reshape(128, 1536)
        second = gh[r, 1].reshape(128, 1536)
        total = jnp.dot(first, wt[0], preferred_element_type=F32)
        total += jnp.dot(second, wt[1], preferred_element_type=F32)
        ig[r] = total.astype(BF16)
        if r:
            copy("ix", r - 1, ig.at[r], irx.at[r - 1], at_x(OFFSET[r]))

    def in_sum():
        for r in range(1, 4):
            arrived("ix", r - 1)
        total = ig[0].astype(F32) + irx[0].astype(F32) + irx[1].astype(F32) + irx[2].astype(F32)
        isum[...] = total.astype(BF16).reshape(4, 32, 768)
        for d in range(1, 4):
            copy("iz", d - 1, isum.at[lax.rem(z + d, 4)], irz.at[d - 1], at_z(d))

    def in_final():
        for d in range(1, 4):
            arrived("iz", d - 1)
        ig_ref[:, own_half] = (isum[z].astype(F32) + irz[1].astype(F32)).astype(BF16)
        ig_ref[:, other_half] = (irz[0].astype(F32) + irz[2].astype(F32)).astype(BF16)

    def transpose_in():
        for r in range(4):
            xgt[:, pl.ds(r * 128, 128)] = xg[r].reshape(128, 768).T

    def transpose_first():
        @pl.loop(0, 6)
        def _(t):
            cols = pl.ds(pl.multiple_of(t * 512, 512), 512)
            spot = pl.ds(pl.multiple_of(lax.rem(t, 3) * 512, 512), 512)
            wt[t // 3, spot] = w1[:, cols].T

    def transpose_second():
        @pl.loop(0, 6)
        def _(t):
            cols = pl.ds(pl.multiple_of(lax.rem(t, 3) * 512, 512), 512)
            some = pl.ds(pl.multiple_of(t // 3 * 768, 768), 768)
            wt[t // 3, cols] = w2[some, cols].T

    def first_grad(half, whose, early):
        core_rows = pl.ds(pl.multiple_of((c if whose else 1 - c) * 384, 128), 384)
        lhs = xgt[core_rows, pl.ds(256 if early else 0, 256)]
        slots = pl.ds(2 if early else 0, 2)
        if whose and not early:
            arrived("fg", half)

        wide = pl.ds(half * 1536, 1536)
        some = gh[slots, half].reshape(256, 1536)
        total = jnp.dot(lhs, some, preferred_element_type=F32)
        if whose:
            if not early:
                total += fg_ref[:, wide].astype(F32) + fgr[half].astype(F32)
            fg_ref[:, wide] = total.astype(BF16)
        else:
            if not early:
                total += gone[half].astype(F32)
            gone[half] = total.astype(BF16)

        if not whose and not early:
            copy("fg", half, gone.at[half], fgr.at[half], core)

    pre_product(0)
    pass_on("xx", "xf", xg, 1)
    pass_on("xx", "xf", xg, 0)
    load_cot.wait()
    for k in range(3):
        arrived("cz", k)
    spread("cx", cotg)
    pre_product(3)
    pre_product(2)
    pre_forward(0)
    arrived("xf", 0)
    arrived("xf", 1)
    pre_product(1)
    load_w2.wait()
    arrived("w2", 0)
    transpose_second()
    pre_forward(3)
    pre_forward(1)
    pre_sum(0)
    pass_on("cx", "cf", cotg, 1)
    pass_on("cx", "cf", cotg, 0)
    grad_product(3)
    grad_product(2)
    pre_cross(2)
    pre_sum(3)
    gelu(0)
    grad_forward(3)
    pre_sum(1)
    gelu(3)
    arrived("cf", 0)
    arrived("cf", 1)
    grad_product(1)
    grad_product(0)
    pre_forward(2)
    grad_forward(2)
    act_send(3)
    act_send(0)
    gelu(1)
    act_send(1)
    hidden_grad(3)
    transpose_in()
    transpose_first()
    grad_forward(1)
    pre_sum(2)
    gelu(2)
    act_send(2)
    hidden_grad(2)
    grad_forward(0)
    act_forward(3)
    act_forward(0)
    hidden_grad(1)
    act_forward(1)
    hid_forward(3, 0)
    hidden_grad(0)
    hidden_pair(1)
    act_forward(2)
    out_product(3)
    hid_forward(2, 0)
    hidden_pair(0)
    out_product(1)
    hid_rest(3)
    out_product(2)
    hid_forward(1, 0)
    hid_rest(2)
    out_product(0)
    hid_forward(0, 0)
    second_grad()
    hid_forward(1, 1)
    in_product(3)
    out_sum()
    hid_forward(0, 1)
    second_grad_own()
    in_product(2)
    for half in range(2):
        first_grad(half, 0, True)
    for half in range(2):
        first_grad(half, 1, True)
    out_final()
    in_product(1)
    in_product(0)
    in_sum()
    for half in range(2):
        first_grad(half, 0, False)
    in_final()
    for half in range(2):
        first_grad(half, 1, False)
    for made in sent.values():
        made.wait_send()


def leave(*refs):
    sems = refs[-1]
    copies = [pltpu.make_async_copy(refs[i], refs[4 + i], sems.at[i]) for i in range(4)]
    for made in copies:
        made.start()
    for made in copies:
        made.wait()


def shards(inputs, first_weight, second_weight, cotangent):
    def vmem(*shape, dtype=BF16):
        return pltpu.VMEM(shape, dtype)

    anywhere = pl.BlockSpec(memory_space=pl.ANY)
    inside = pl.BlockSpec(memory_space=pltpu.VMEM)
    shapes = [(32, 1536), (32, 1536), (384, 3072), (768, 1536)]
    results = pl.pallas_call(
        kernel,
        out_shape=[pltpu.VMEM(shape, BF16) for shape in shapes],
        in_specs=[anywhere] * 4,
        out_specs=[inside] * 4,
        scratch_shapes=[
            vmem(768, 3072), vmem(1536, 1536), vmem(2, 1536, 768), vmem(4, 4, 32, 768), vmem(768, 512), vmem(4, 4, 32, 1536),
            vmem(4, 2, 128, 1536), vmem(4, 2, 2, 16, 1536), vmem(4, 2, 2, 16, 1536), vmem(4, 2, 2, 16, 1536),
            vmem(4, 32, 1536), vmem(4, 32, 1536), vmem(len(PRE_CROSS), 128, 1536),
            vmem(4, 128, 1536), vmem(4, 2, 16, 1536), vmem(4, 2, 16, 1536), vmem(4, 2, 16, 1536),
            vmem(4, 32, 1536, dtype=F32), vmem(4, 4, 32, 1536), vmem(1536, 512), vmem(4, 2, 4, 32, 1536),
            vmem(3, 128, 1536), vmem(4, 32, 1536), vmem(3, 32, 1536),
            vmem(4, 128, 768), vmem(3, 128, 768), vmem(4, 32, 768), vmem(3, 32, 768),
            vmem(2, 384, 1536), vmem(2, 384, 1536), vmem(2, 384, 1536),
            pltpu.SemaphoreType.DMA((N_MESSAGES,)),
            pltpu.SemaphoreType.DMA((N_MESSAGES,)),
            pltpu.SemaphoreType.DMA((4,)),
        ],
        compiler_params=pltpu.CompilerParams(
            collective_id=0, has_side_effects=True, vmem_limit_bytes=50 << 20
        ),
        name="layer",
    )(inputs, first_weight, second_weight, cotangent)
    results = [pltpu.with_memory_space_constraint(result, pltpu.VMEM) for result in results]
    return pl.pallas_call(
        leave,
        out_shape=[jax.ShapeDtypeStruct(shape, BF16) for shape in shapes],
        in_specs=[inside] * 4,
        out_specs=[anywhere] * 4,
        scratch_shapes=[pltpu.SemaphoreType.DMA((4,))],
        compiler_params=pltpu.CompilerParams(vmem_limit_bytes=1 << 20),
        name="leave",
    )(*results)


def solution(mesh):
    in_specs = (
        P(("ia", "al"), "ja"),
        P(("ja", "ia"), "al"),
        P(("al", "ia"), "ja"),
        P(("ia", "al"), "ja"),
    )
    out_specs = (
        P(("ia", "al"), "ja"),
        P(("ia", "al"), "ja"),
        P(("ja", "ia"), "al"),
        P(("al", "ia"), "ja"),
    )
    return jax.shard_map(shards, mesh=mesh, in_specs=in_specs, out_specs=out_specs, check_vma=False)
```

time: 132 us -> 111 us (0.84); the launches traced: 130 us -> 111 us
  Pallas kernels: 121 us -> 110 us
  local copies, waits for them, and re-layouts: 7.86 us -> 0 us
    pallas_call x1 -> x2, Pallas kernels: 121 us -> 110 us  [the longest x1 108 us: shards(): pl.pallas_call(kernel, out_shape=[pltpu.VMEM(shape, BF16) for shape in sh...]
    unnamed x6 -> x0, local copies, waits for them, and re-layouts: 7.86 us -> none
where the time goes in v3:
time: 111 us
  Pallas kernels  110 us (99%)
    pallas_call x1, Pallas kernels, shards(): pl.pallas_call(kernel, out_shape=[pltpu.VMEM(shape, BF16) for shape in sh...  108 us
    pallas_call x1, Pallas kernels, shards(): pl.pallas_call(leave, out_shape=[jax.ShapeDtypeStruct(shape, BF16) for sh...  2.28 us

profile of v3, /device:TPU:1, one launch (start us, length us, event | category | flops | bytes accessed | tf_op | source)
XLA Modules:
  0.0 110.7 jit_solution(12420299909512155733)
XLA Ops:
  0.6 107.6 %layer.1 = (bf16[32,1536]{1,0:T(8,128)(2,1)S(1)}, bf16[32,1536]{1,0:T(8,128)(2,1)S(1)}, bf16[384,3072]{1,0:T(8,128)(2,1)S(1)}, bf16[768,1536]{1,0:T(8,128)(2,1)S(1)}) custom-call(bf16[32,1536]{1,0:T(8,128)(2,1)} %x_ref.1, bf16[384,3072]{1,0:T(8,128)(2,1)} %w1_ref.1, bf16[768,1536]{1,0:T(8,128)(2,1)} %w2_ref.1, bf16[32,1536]{1,0:T(8,128)(2,1)} %cot_ref.1), custom_call_target="tpu_custom_call" | custom-call | tf_op jit(solution)/shard_map/layer/pallas_call | solution.py:505
  108.3 2.3 %leave.1 = (bf16[32,1536]{1,0:T(8,128)(2,1)}, bf16[32,1536]{1,0:T(8,128)(2,1)}, bf16[384,3072]{1,0:T(8,128)(2,1)}, bf16[768,1536]{1,0:T(8,128)(2,1)}) custom-call(bf16[32,1536]{1,0:T(8,128)(2,1)S(1)} %get-tuple-element.8.refs_0_, bf16[32,1536]{1,0:T(8,128)(2,1)S(1)} %get-tuple-element.9.refs_1_, bf16[384,3072]{1,0:T(8,128)(2,1)S(1)} %get-tuple-element.10.refs_2_, ...), custom_call_target="tpu_custom_call" | custom-call | tf_op jit(solution)/shard_map/leave/pallas_call | solution.py:529

commit v4 on v3

--- a/solution.py
+++ b/solution.py
@@ -10,8 +10,8 @@
 
 OFFSET = (0, 2, 1, 3)
 SLOT = {offset: slot for slot, offset in enumerate(OFFSET)}
-PRE_CROSS = (2,)
-HID_CROSS = (2, 3)
+PRE_CROSS = (2, 1)
+HID_CROSS = (1, 3)
 
 
 def gelu_parts(pre):
@@ -399,89 +399,90 @@
     pre_product(0)
     pass_on("xx", "xf", xg, 1)
     pass_on("xx", "xf", xg, 0)
+    load_w2.wait()
+    arrived("w2", 0)
+    pre_product(3)
+    pre_forward(0)
     load_cot.wait()
     for k in range(3):
         arrived("cz", k)
     spread("cx", cotg)
-    pre_product(3)
-    pre_product(2)
-    pre_forward(0)
+    transpose_second()
+    grad_product(0)
     arrived("xf", 0)
     arrived("xf", 1)
     pre_product(1)
-    load_w2.wait()
-    arrived("w2", 0)
-    transpose_second()
     pre_forward(3)
-    pre_forward(1)
-    pre_sum(0)
+    grad_forward(0)
+    pre_product(2)
     pass_on("cx", "cf", cotg, 1)
+    grad_product(3)
     pass_on("cx", "cf", cotg, 0)
-    grad_product(3)
     grad_product(2)
-    pre_cross(2)
-    pre_sum(3)
-    gelu(0)
+    pre_cross(1)
     grad_forward(3)
-    pre_sum(1)
-    gelu(3)
+    grad_forward(2)
+    transpose_in()
     arrived("cf", 0)
     arrived("cf", 1)
+    pre_sum(3)
+    pre_forward(1)
     grad_product(1)
-    grad_product(0)
-    pre_forward(2)
-    grad_forward(2)
-    act_send(3)
-    act_send(0)
+    transpose_first()
+    pre_cross(2)
+    pre_sum(1)
     gelu(1)
     act_send(1)
-    hidden_grad(3)
-    transpose_in()
-    transpose_first()
+    gelu(3)
     grad_forward(1)
+    pre_sum(0)
+    pre_forward(2)
+    act_send(3)
+    act_forward(1)
+    hidden_grad(1)
     pre_sum(2)
     gelu(2)
     act_send(2)
+    act_forward(3)
+    hidden_grad(3)
+    gelu(0)
+    out_product(1)
+    hid_forward(1, 0)
+    act_forward(2)
+    act_send(0)
     hidden_grad(2)
-    grad_forward(0)
-    act_forward(3)
+    hid_rest(1)
+    hid_forward(3, 0)
+    out_product(3)
+    out_product(2)
     act_forward(0)
-    hidden_grad(1)
-    act_forward(1)
-    hid_forward(3, 0)
+    hidden_pair(2)
     hidden_grad(0)
-    hidden_pair(1)
-    act_forward(2)
-    out_product(3)
     hid_forward(2, 0)
+    in_product(1)
+    hid_rest(3)
+    out_product(0)
+    second_grad()
+    hid_forward(2, 1)
     hidden_pair(0)
-    out_product(1)
-    hid_rest(3)
-    out_product(2)
-    hid_forward(1, 0)
-    hid_rest(2)
-    out_product(0)
     hid_forward(0, 0)
-    second_grad()
-    hid_forward(1, 1)
     in_product(3)
+    in_product(2)
     out_sum()
     hid_forward(0, 1)
     second_grad_own()
-    in_product(2)
     for half in range(2):
         first_grad(half, 0, True)
+    in_product(0)
+    for half in range(2):
+        first_grad(half, 0, False)
+    in_sum()
+    out_final()
     for half in range(2):
         first_grad(half, 1, True)
-    out_final()
-    in_product(1)
-    in_product(0)
-    in_sum()
-    for half in range(2):
-        first_grad(half, 0, False)
-    in_final()
     for half in range(2):
         first_grad(half, 1, False)
+    in_final()
     for made in sent.values():
         made.wait_send()
 

time: 111 us -> 94.4 us (0.85)
  Pallas kernels: 110 us -> 93.5 us
    pallas_call x1, Pallas kernels: 108 us -> 91.2 us  [shards(): pl.pallas_call(kernel, out_shape=[pltpu.VMEM(shape, BF16) for shape in sh...]
where the time goes in v4:
time: 94.4 us; the launch traced here: 94.3 us
  Pallas kernels  93.5 us (99%)
    pallas_call x1, Pallas kernels, shards(): pl.pallas_call(kernel, out_shape=[pltpu.VMEM(shape, BF16) for shape in sh...  91.2 us
    pallas_call x1, Pallas kernels, shards(): pl.pallas_call(leave, out_shape=[jax.ShapeDtypeStruct(shape, BF16) for sh...  2.28 us

profile of v4, /device:TPU:1, one launch (start us, length us, event | category | flops | bytes accessed | tf_op | source)
XLA Modules:
  0.0 94.3 jit_solution(17043385743885161395)
XLA Ops:
  0.6 91.2 %layer.1 = (bf16[32,1536]{1,0:T(8,128)(2,1)S(1)}, bf16[32,1536]{1,0:T(8,128)(2,1)S(1)}, bf16[384,3072]{1,0:T(8,128)(2,1)S(1)}, bf16[768,1536]{1,0:T(8,128)(2,1)S(1)}) custom-call(bf16[32,1536]{1,0:T(8,128)(2,1)} %x_ref.1, bf16[384,3072]{1,0:T(8,128)(2,1)} %w1_ref.1, bf16[768,1536]{1,0:T(8,128)(2,1)} %w2_ref.1, bf16[32,1536]{1,0:T(8,128)(2,1)} %cot_ref.1), custom_call_target="tpu_custom_call" | custom-call | tf_op jit(solution)/shard_map/layer/pallas_call | solution.py:506
  91.8 2.3 %leave.1 = (bf16[32,1536]{1,0:T(8,128)(2,1)}, bf16[32,1536]{1,0:T(8,128)(2,1)}, bf16[384,3072]{1,0:T(8,128)(2,1)}, bf16[768,1536]{1,0:T(8,128)(2,1)}) custom-call(bf16[32,1536]{1,0:T(8,128)(2,1)S(1)} %get-tuple-element.8.refs_0_, bf16[32,1536]{1,0:T(8,128)(2,1)S(1)} %get-tuple-element.9.refs_1_, bf16[384,3072]{1,0:T(8,128)(2,1)S(1)} %get-tuple-element.10.refs_2_, ...), custom_call_target="tpu_custom_call" | custom-call | tf_op jit(solution)/shard_map/leave/pallas_call | solution.py:530

commit v5 on v4

--- a/solution.py
+++ b/solution.py
@@ -11,7 +11,7 @@
 OFFSET = (0, 2, 1, 3)
 SLOT = {offset: slot for slot, offset in enumerate(OFFSET)}
 PRE_CROSS = (2, 1)
-HID_CROSS = (1, 3)
+HID_CROSS = (1, 2, 3)
 
 
 def gelu_parts(pre):
@@ -31,7 +31,7 @@
 
 
 LAYOUT = [
-    ("xz", 3), ("xx", 2), ("xf", 2), ("cz", 3), ("cx", 2), ("cf", 2), ("w1", 1), ("w2", 1),
+    ("xz", 3), ("xx", 8), ("xf", 2), ("cz", 3), ("cx", 2), ("cf", 2), ("w1", 1), ("w2", 1),
     ("pa", 8), ("pb", 8), ("pc", 8), ("pz", 4),
     ("ga", 8), ("gb", 8), ("gc", 8),
     ("as", 8), ("af", 8), ("hz", 20), ("hs", 16), ("hf", 16),
@@ -124,16 +124,22 @@
         copy(name, 0, buffer.at[0], buffer.at[SLOT[1]], at_x(3))
         copy(name, 1, buffer.at[0], buffer.at[SLOT[3]], at_x(1))
 
+    def spread_block(k, block):
+        copy("xx", k, xg.at[0, block], xg.at[SLOT[1], block], at_x(3))
+        copy("xx", 4 + k, xg.at[0, block], xg.at[SLOT[3], block], at_x(1))
+
     def pass_on(name, far, buffer, side):
-        arrived(name, side)
+        for k in range(4 * side, 4 * side + 4) if name == "xx" else (side,):
+            arrived(name, k)
         slot, half, device = ((SLOT[1], 0, at_x(3)), (SLOT[3], 2, at_x(1)))[side]
         part = pl.ds(half, 2)
         copy(far, side, buffer.at[slot, part], buffer.at[SLOT[2], part], device)
 
     load_x.wait()
-    for k in range(3):
-        arrived("xz", k)
-    spread("xx", xg)
+    spread_block(0, z)
+    for k, (message, step) in enumerate(((0, 3), (2, 1), (1, 2))):
+        arrived("xz", message)
+        spread_block(k + 1, lax.rem(z + step, 4))
     load_w1.wait()
     arrived("w1", 0)
 
@@ -376,13 +382,14 @@
 
     def first_grad(half, whose, early):
         core_rows = pl.ds(pl.multiple_of((c if whose else 1 - c) * 384, 128), 384)
-        lhs = xgt[core_rows, pl.ds(256 if early else 0, 256)]
-        slots = pl.ds(2 if early else 0, 2)
+        depth = 384 if early else 128
+        lhs = xgt[core_rows, pl.ds(128 if early else 0, depth)]
+        slots = pl.ds(1, 3) if early else pl.ds(0, 1)
         if whose and not early:
             arrived("fg", half)
 
         wide = pl.ds(half * 1536, 1536)
-        some = gh[slots, half].reshape(256, 1536)
+        some = gh[slots, half].reshape(depth, 1536)
         total = jnp.dot(lhs, some, preferred_element_type=F32)
         if whose:
             if not early:
@@ -397,89 +404,88 @@
             copy("fg", half, gone.at[half], fgr.at[half], core)
 
     pre_product(0)
+    pass_on("xx", "xf", xg, 0)
+    pre_product(2)
     pass_on("xx", "xf", xg, 1)
-    pass_on("xx", "xf", xg, 0)
-    load_w2.wait()
-    arrived("w2", 0)
     pre_product(3)
     pre_forward(0)
     load_cot.wait()
     for k in range(3):
         arrived("cz", k)
     spread("cx", cotg)
+    load_w2.wait()
+    arrived("w2", 0)
     transpose_second()
-    grad_product(0)
     arrived("xf", 0)
     arrived("xf", 1)
+    grad_product(0)
     pre_product(1)
     pre_forward(3)
-    grad_forward(0)
-    pre_product(2)
-    pass_on("cx", "cf", cotg, 1)
-    grad_product(3)
+    pre_cross(2)
     pass_on("cx", "cf", cotg, 0)
     grad_product(2)
+    pass_on("cx", "cf", cotg, 1)
+    pre_forward(2)
+    grad_product(3)
+    grad_forward(2)
     pre_cross(1)
-    grad_forward(3)
-    grad_forward(2)
-    transpose_in()
+    pre_sum(3)
+    pre_sum(0)
     arrived("cf", 0)
     arrived("cf", 1)
-    pre_sum(3)
+    pre_sum(2)
+    gelu(2)
+    grad_product(1)
     pre_forward(1)
-    grad_product(1)
+    gelu(3)
+    hidden_grad(2)
     transpose_first()
-    pre_cross(2)
+    grad_forward(1)
     pre_sum(1)
     gelu(1)
     act_send(1)
-    gelu(3)
-    grad_forward(1)
-    pre_sum(0)
-    pre_forward(2)
     act_send(3)
+    hid_forward(2, 0)
     act_forward(1)
     hidden_grad(1)
-    pre_sum(2)
-    gelu(2)
     act_send(2)
-    act_forward(3)
-    hidden_grad(3)
     gelu(0)
+    hid_rest(2)
     out_product(1)
+    grad_forward(3)
     hid_forward(1, 0)
     act_forward(2)
+    act_forward(3)
+    grad_forward(0)
+    hid_rest(1)
+    hidden_grad(3)
     act_send(0)
-    hidden_grad(2)
-    hid_rest(1)
+    out_product(2)
+    out_product(3)
+    hidden_grad(0)
     hid_forward(3, 0)
-    out_product(3)
-    out_product(2)
+    in_product(1)
     act_forward(0)
-    hidden_pair(2)
-    hidden_grad(0)
-    hid_forward(2, 0)
-    in_product(1)
+    in_product(2)
+    hidden_pair(0)
     hid_rest(3)
+    hid_forward(0, 0)
+    transpose_in()
     out_product(0)
     second_grad()
-    hid_forward(2, 1)
-    hidden_pair(0)
-    hid_forward(0, 0)
+    hid_forward(0, 1)
     in_product(3)
-    in_product(2)
     out_sum()
-    hid_forward(0, 1)
+    in_product(0)
     second_grad_own()
     for half in range(2):
         first_grad(half, 0, True)
-    in_product(0)
+    in_sum()
     for half in range(2):
         first_grad(half, 0, False)
-    in_sum()
-    out_final()
     for half in range(2):
         first_grad(half, 1, True)
+    out_final()
     for half in range(2):
         first_grad(half, 1, False)
     in_final()

time: 94.4 us -> 94.3 us (level)
  no operation moved by 1% of the time
where the time goes in v5:
time: 94.3 us; the launch traced here: 94.2 us
  Pallas kernels  93.4 us (99%)
    pallas_call x1, Pallas kernels, shards(): pl.pallas_call(kernel, out_shape=[pltpu.VMEM(shape, BF16) for shape in sh...  91.1 us
    pallas_call x1, Pallas kernels, shards(): pl.pallas_call(leave, out_shape=[jax.ShapeDtypeStruct(shape, BF16) for sh...  2.28 us

profile of v5, /device:TPU:1, one launch (start us, length us, event | category | flops | bytes accessed | tf_op | source)
XLA Modules:
  0.0 94.2 jit_solution(12424721842777739773)
XLA Ops:
  0.6 91.1 %layer.1 = (bf16[32,1536]{1,0:T(8,128)(2,1)S(1)}, bf16[32,1536]{1,0:T(8,128)(2,1)S(1)}, bf16[384,3072]{1,0:T(8,128)(2,1)S(1)}, bf16[768,1536]{1,0:T(8,128)(2,1)S(1)}) custom-call(bf16[32,1536]{1,0:T(8,128)(2,1)} %x_ref.1, bf16[384,3072]{1,0:T(8,128)(2,1)} %w1_ref.1, bf16[768,1536]{1,0:T(8,128)(2,1)} %w2_ref.1, bf16[32,1536]{1,0:T(8,128)(2,1)} %cot_ref.1), custom_call_target="tpu_custom_call" | custom-call | tf_op jit(solution)/shard_map/layer/pallas_call | solution.py:512
  91.7 2.3 %leave.1 = (bf16[32,1536]{1,0:T(8,128)(2,1)}, bf16[32,1536]{1,0:T(8,128)(2,1)}, bf16[384,3072]{1,0:T(8,128)(2,1)}, bf16[768,1536]{1,0:T(8,128)(2,1)}) custom-call(bf16[32,1536]{1,0:T(8,128)(2,1)S(1)} %get-tuple-element.8.refs_0_, bf16[32,1536]{1,0:T(8,128)(2,1)S(1)} %get-tuple-element.9.refs_1_, bf16[384,3072]{1,0:T(8,128)(2,1)S(1)} %get-tuple-element.10.refs_2_, ...), custom_call_target="tpu_custom_call" | custom-call | tf_op jit(solution)/shard_map/leave/pallas_call | solution.py:536

commit v6 on v5

--- a/solution.py
+++ b/solution.py
@@ -32,7 +32,7 @@
 
 LAYOUT = [
     ("xz", 3), ("xx", 8), ("xf", 2), ("cz", 3), ("cx", 2), ("cf", 2), ("w1", 1), ("w2", 1),
-    ("pa", 8), ("pb", 8), ("pc", 8), ("pz", 4),
+    ("pa", 8), ("pb", 8), ("pc", 8), ("pz", 4), ("qa", 4), ("qb", 4),
     ("ga", 8), ("gb", 8), ("gc", 8),
     ("as", 8), ("af", 8), ("hz", 20), ("hs", 16), ("hf", 16),
     ("ox", 3), ("oz", 3), ("ix", 3), ("iz", 3), ("sg", 1), ("fg", 2),
@@ -152,11 +152,26 @@
         for half in range(2):
             cols = pl.ds(half * 1536, 1536)
             p[r, half] = jnp.dot(lhs, w1[:, cols], preferred_element_type=F32).astype(BF16)
+            if r == 0:
+                pre_send_half(half)
 
         if r in PRE_CROSS:
             copy("pz", r, p.at[r, 1 - zl], prc.at[PRE_CROSS.index(r)], pair)
+        elif r:
+            pre_send(r)
+
+    def pre_send_half(half):
+        copy("qa", half, p.at[0, half, rows(y2, 0)], pa.at[0, 0, half], at_y(3))
+        copy("qa", 2 + half, p.at[0, half, rows(y2, 1)], pa.at[0, 1, half], at_y(1))
+        copy("qb", half, p.at[0, half, rows(y3, 1)], pb.at[0, 0, half], at_y(3))
+        copy("qb", 2 + half, p.at[0, half, rows(y1, 0)], pb.at[0, 1, half], at_y(1))
+
+    def pre_arrived(name, r, side):
+        if r:
+            arrived("p" + name, 2 * r + side)
         else:
-            pre_send(r)
+            arrived("q" + name, 2 * side)
+            arrived("q" + name, 2 * side + 1)
 
     def pre_view(r):
         return p.at[r, pl.ds(zl, 1)] if r in PRE_CROSS else p.at[r]
@@ -184,7 +199,7 @@
     def pre_forward(r):
         mine = pre_view(r)
         for side, (block, half, device) in enumerate(((y3, 0, at_y(3)), (y1, 1, at_y(1)))):
-            arrived("pa", 2 * r + side)
+            pre_arrived("a", r, side)
             spot = rows(block, half)
             mine[:, spot] = (mine[:, spot].astype(F32) + pre_room(pa, r, side)[...].astype(F32)).astype(BF16)
             copy("pc", 2 * r + side, mine.at[:, spot], pre_room(pc, r, side), device)
@@ -197,7 +212,7 @@
 
     def pre_sum(r):
         for side in range(2):
-            arrived("pb", 2 * r + side)
+            pre_arrived("b", r, side)
             arrived("pc", 2 * r + side)
         if r not in PRE_CROSS:
             ps[r] = pre_block(r, 1 - zl).astype(BF16)

time: 94.3 us -> 94 us (level)
  no operation moved by 1% of the time
where the time goes in v6:
time: 94 us; the launch traced here: 93.9 us
  Pallas kernels  93.1 us (99%)
    pallas_call x1, Pallas kernels, shards(): pl.pallas_call(kernel, out_shape=[pltpu.VMEM(shape, BF16) for shape in sh...  90.8 us
    pallas_call x1, Pallas kernels, shards(): pl.pallas_call(leave, out_shape=[jax.ShapeDtypeStruct(shape, BF16) for sh...  2.28 us

profile of v6, /device:TPU:1, one launch (start us, length us, event | category | flops | bytes accessed | tf_op | source)
XLA Modules:
  0.0 93.9 jit_solution(11919050016419708704)
XLA Ops:
  0.6 90.8 %layer.1 = (bf16[32,1536]{1,0:T(8,128)(2,1)S(1)}, bf16[32,1536]{1,0:T(8,128)(2,1)S(1)}, bf16[384,3072]{1,0:T(8,128)(2,1)S(1)}, bf16[768,1536]{1,0:T(8,128)(2,1)S(1)}) custom-call(bf16[32,1536]{1,0:T(8,128)(2,1)} %x_ref.1, bf16[384,3072]{1,0:T(8,128)(2,1)} %w1_ref.1, bf16[768,1536]{1,0:T(8,128)(2,1)} %w2_ref.1, bf16[32,1536]{1,0:T(8,128)(2,1)} %cot_ref.1), custom_call_target="tpu_custom_call" | custom-call | tf_op jit(solution)/shard_map/layer/pallas_call | solution.py:527
  91.5 2.3 %leave.1 = (bf16[32,1536]{1,0:T(8,128)(2,1)}, bf16[32,1536]{1,0:T(8,128)(2,1)}, bf16[384,3072]{1,0:T(8,128)(2,1)}, bf16[768,1536]{1,0:T(8,128)(2,1)}) custom-call(bf16[32,1536]{1,0:T(8,128)(2,1)S(1)} %get-tuple-element.8.refs_0_, bf16[32,1536]{1,0:T(8,128)(2,1)S(1)} %get-tuple-element.9.refs_1_, bf16[384,3072]{1,0:T(8,128)(2,1)S(1)} %get-tuple-element.10.refs_2_, ...), custom_call_target="tpu_custom_call" | custom-call | tf_op jit(solution)/shard_map/leave/pallas_call | solution.py:551
